TPU v7x, 32 devices: a whole 2x2x4 slice. The times are simulated.
32 devices in a mesh: grp: 2 (over x), tm: 16 (over z, y, core).
Axes of the slice: x: 2, y: 2, z: 4, core: 2. Of those that a mesh axis runs over, the one named last changes fastest.
Arguments:
- density: float32 [32, 512, 512], P(('grp', 'tm')), parts along dimension 0, may hold values from 0.25 to 2.5
- flux_x: float32 [32, 512, 512], P(('grp', 'tm')), parts along dimension 0, may hold values from -5 to 5
- flux_y: float32 [32, 512, 512], P(('grp', 'tm')), parts along dimension 0, may hold values from -5 to 5
- potential: float32 [32, 512, 512], P(('grp', 'tm')), parts along dimension 0, may hold values from -6 to 6
- initial_density: float32 [1024, 512], P('grp'), parts along dimension 0, may hold values from 0.25 to 2.5
- running_cost: float32 [1024, 512], P('grp'), parts along dimension 0, may hold values from 0 to 1.5
Outputs:
- density_out: float32 [32, 512, 512], P(('grp', 'tm')), parts along dimension 0
- flux_x_out: float32 [32, 512, 512], P(('grp', 'tm')), parts along dimension 0
- flux_y_out: float32 [32, 512, 512], P(('grp', 'tm')), parts along dimension 0
- potential_out: float32 [32, 512, 512], P(('grp', 'tm')), parts along dimension 0
There are 2 independent parts, one for each index of `grp`. A program takes and returns all parts, laid end to end along the dimension named above; each array names one. Nothing has to cross between parts.
All inputs are finite; a program needn't handle non-finite values.
Results may differ from a plain program's by a relative error of at most 0.00018.
Values sent between devices are 32-bit elements; how exact they have to be, the bound alone decides.
A program may use at most 64 MiB of HBM per device.

v0:
```python
import jax
import jax.numpy as jnp
from jax import lax
from jax.sharding import PartitionSpec as P

ITERS = 2
NEWTON = 3


PRIMAL_STEP = 0.5
DUAL_STEP = 0.5
CONGESTION = 0.1
SCREENING = 0.05


def from_behind(value, axis, steps):
    count = lax.axis_size(axis)
    first, last = (max(0, -steps), min(count, count - steps))
    return lax.ppermute(value, axis, [(source, source + steps) for source in range(first, last)])


def cosine_table(length):
    freq = jnp.arange(length, dtype=jnp.float32)[:, None]
    place = jnp.arange(length, dtype=jnp.float32)[None, :]
    scale = jnp.where(freq == 0, jnp.sqrt(1.0 / length), jnp.sqrt(2.0 / length))
    return scale * jnp.cos(jnp.pi * (place + 0.5) * freq / length)


def spectrum(length):
    return 2.0 - 2.0 * jnp.cos(jnp.pi * jnp.arange(length, dtype=jnp.float32) / length)


def forward_diff(values, dimension):
    differences = jnp.diff(values, axis=dimension)
    widths = [(0, 0), (0, 0), (0, 0)]
    widths[dimension] = (0, 1)
    return jnp.pad(differences, widths)


def backward_div(flux_part, dimension):
    count = flux_part.shape[dimension]
    kept = lax.slice_in_dim(flux_part, 0, count - 1, axis=dimension)
    after = [(0, 0), (0, 0), (0, 0)]
    after[dimension] = (0, 1)
    before = [(0, 0), (0, 0), (0, 0)]
    before[dimension] = (1, 0)
    return jnp.pad(kept, after) - jnp.pad(kept, before)


def proximal(density, flux_x, flux_y, time_grad, grad_x, grad_y, running_cost):
    moment_x = flux_x + PRIMAL_STEP * grad_x
    moment_y = flux_y + PRIMAL_STEP * grad_y
    kinetic = 0.5 * PRIMAL_STEP * (moment_x * moment_x + moment_y * moment_y)
    slope = 1.0 + CONGESTION * PRIMAL_STEP
    offset = density + PRIMAL_STEP * (time_grad - running_cost)
    guess = jnp.maximum(offset / slope, 0.0) + jnp.cbrt(kinetic / slope)
    for sweep in range(NEWTON):
        shifted = guess + PRIMAL_STEP
        linear = slope * guess - offset
        residue = linear * shifted * shifted - kinetic
        derivative = slope * shifted * shifted + 2.0 * linear * shifted
        guess = jnp.maximum(guess - residue / derivative, 0.0)
    weight = guess / (guess + PRIMAL_STEP)
    return (guess, weight * moment_x, weight * moment_y)


def local(density, flux_x, flux_y, potential, initial_density, running_cost):
    slices, rows_all, cols_all = density.shape
    devices = lax.axis_size("tm")
    position = lax.axis_index("tm")
    strip = rows_all // devices
    times = slices * devices
    highest = lax.Precision.HIGHEST
    table_t = cosine_table(times)
    table_x = cosine_table(rows_all)
    table_y = cosine_table(cols_all)
    strip_spectrum = lax.dynamic_slice_in_dim(spectrum(rows_all), position * strip, strip)
    denominator = (
        SCREENING
        + spectrum(times)[:, None, None]
        + strip_spectrum[None, :, None]
        + spectrum(cols_all)[None, None, :]
    )
    cost_field = running_cost[None]
    final_slice = ((jnp.arange(slices) == slices - 1) & (position == devices - 1))[:, None, None]
    for sweep in range(ITERS):
        following = from_behind(potential[:1], "tm", -1)
        extended = jnp.concatenate([potential, following], axis=0)
        time_grad = jnp.where(final_slice, 0.0, extended[1:] - extended[:-1])
        grad_x = forward_diff(potential, 1)
        grad_y = forward_diff(potential, 2)
        new_density, new_x, new_y = proximal(
            density, flux_x, flux_y, time_grad, grad_x, grad_y, cost_field
        )
        bar_density = 2.0 * new_density - density
        bar_x = 2.0 * new_x - flux_x
        bar_y = 2.0 * new_y - flux_y
        prev_bar = from_behind(bar_density[-1:], "tm", 1)
        prev_bar = jnp.where(position == 0, initial_density[None], prev_bar)
        previous = jnp.concatenate([prev_bar, bar_density[:-1]], axis=0)
        source = bar_density - previous + backward_div(bar_x, 1) + backward_div(bar_y, 2)
        spectral = jnp.einsum("ax,txy->tay", table_x, source, precision=highest)
        spectral = jnp.einsum("txy,by->txb", spectral, table_y, precision=highest)
        gathered = lax.all_to_all(spectral, "tm", split_axis=1, concat_axis=0, tiled=True)
        modes = jnp.einsum("kt,txy->kxy", table_t, gathered, precision=highest)
        modes = modes / denominator
        solved = jnp.einsum("kt,kxy->txy", table_t, modes, precision=highest)
        returned = lax.all_to_all(solved, "tm", split_axis=0, concat_axis=1, tiled=True)
        field = jnp.einsum("ax,tay->txy", table_x, returned, precision=highest)
        field = jnp.einsum("txb,by->txy", field, table_y, precision=highest)
        potential = potential + DUAL_STEP * field
        density, flux_x, flux_y = (new_density, new_x, new_y)
    return (density, flux_x, flux_y, potential)


def solution(mesh):
    in_specs = (
        P(("grp", "tm"), None, None),
        P(("grp", "tm"), None, None),
        P(("grp", "tm"), None, None),
        P(("grp", "tm"), None, None),
        P("grp", None),
        P("grp", None),
    )
    out_specs = (
        P(("grp", "tm"), None, None),
        P(("grp", "tm"), None, None),
        P(("grp", "tm"), None, None),
        P(("grp", "tm"), None, None),
    )
    return jax.shard_map(local, mesh=mesh, in_specs=in_specs, out_specs=out_specs, check_vma=False)
```

profile of v0, /device:TPU:0, one launch (start us, length us, event | category | flops | bytes accessed | tf_op | source)
XLA Modules:
  0.0 267.4 jit_solution(15800189729267185972)
XLA Ops:
  2.0 2.0 slice_subtract_fusion.2
  5.9 5.3 %multiply_subtract_fusion.4 = (f32[1,512,512]{2,1,0:T(8,128)}, f32[1,512,512]{2,1,0:T(8,128)}, f32[1,512,512]{2,1,0:T(8,128)S(1)}) fusion(f32[1,512,512]{2,1,0:T(8,128)S(1)} %copy-done.8, f32[1,511,512]{2,1,0:T(8,128)S(1)} %slice_subtract_fusion.3, f32[1,512,512]{2,1,0:T(8,128)S(1)} %copy-done.1, f32[1,512,511]{2,1,0:T(8,128)S(1)} %slice_subtract_fusion.2, ...), kind=kLoop, calls=%fused_computation.97 | loop fusion | flops 15990784 | bytes 11530241 | tf_op jit(solution)/shard_map/sub | solution.py:96
  11.2 1.9 multiply_subtract_fusion.3
  13.0 15.7 %collective-permute-start.1 = (f32[1,512,512]{2,1,0:T(8,128)}, f32[1,512,512]{2,1,0:T(8,128)}, u32[]{:S(2)}, u32[]{:S(2)}) collective-permute-start(f32[1,512,512]{2,1,0:T(8,128)} %get-tuple-element.15), channel_id=1, source_target_pairs={{0,1},{1,2},{2,3},{3,4},{4,5},{5,6},{6,7},{7,8},{8,9},{9,10},{10,1... | collective-permute-start | bytes 3145736 | tf_op jit(solution)/shard_map/ppermute | solution.py:19
  30.8 10.4 %convolution_bitcast_fusion.5 = f32[512,512]{0,1:T(8,128)S(1)} fusion(f32[1,512,512]{2,1,0:T(8,128)} %get-tuple-element.15, f32[1,512,512]{2,1,0:T(8,128)} %collective-permute-done.1, f32[512,512]{1,0:T(8,128)} %param.10, f32[1,512,511]{2,1,0:T(8,128)} %bitcast.109, f32[1,512,512]{2,1,0:T(8,128)} %get-tuple-element.12, f32[1,511,512]{2,1,0:T(8,128)} %bitcast.108, ...), kind=kOutput, calls=%fused_computation.19 | convolution fusion | flops 1613496320 | bytes 8389121 | tf_op jit(solution)/shard_map/ax,txy->tay/dot_general | solution.py:102
  41.1 7.6 %convolution_bitcast_fusion.4 = f32[1,512,512]{2,1,0:T(8,128)S(1)} fusion(f32[512,512]{0,1:T(8,128)S(1)} %convolution_bitcast_fusion.5, f32[512]{0:T(512)S(1)} %get-tuple-element.16, f32[512]{0:T(512)S(1)} %get-tuple-element.17), kind=kOutput, calls=%fused_computation.18 | convolution fusion | flops 1611399168 | bytes 2101248 | tf_op jit(solution)/shard_map/txy,by->txb/dot_general | solution.py:103
  48.7 2.0 copy.18
  50.8 17.4 %all-to-all-start = ((f32[1,512,512]{2,0,1:T(1,128)}), f32[1,512,512]{2,0,1:T(1,128)}, u32[]{:S(2)}, u32[]{:S(2)}) async-start(f32[1,512,512]{2,0,1:T(1,128)} %copy.18), calls=%async_computation | async-start | bytes 2097152 | tf_op jit(solution)/shard_map/all_to_all | solution.py:104
  68.4 22.7 %all-to-all-done = f32[1,512,512]{2,0,1:T(1,128)} async-done(((f32[1,512,512]{2,0,1:T(1,128)}), f32[1,512,512]{2,0,1:T(1,128)}, u32[]{:S(2)}, u32[]{:S(2)}) %all-to-all-start) | async-done | bytes 1048608 | tf_op jit(solution)/shard_map/all_to_all | solution.py:104
  92.4 1.6 add_divide_fusion.3
  95.8 31.7 %all_to_all.42 = f32[16,32,512]{2,1,0:T(8,128)S(1)} all-to-all(f32[16,32,512]{2,1,0:T(8,128)S(1)} %copy.21), channel_id=1, replica_groups=mesh['grp'=2,'tm'=16] {'tm'}, dimensions={0} | all-to-all | bytes 2097152 | tf_op jit(solution)/shard_map/all_to_all | solution.py:108
  127.5 5.6 %convolution_bitcast_fusion.3 = f32[512,512]{0,1:T(8,128)S(1)} fusion(f32[512,512]{1,0:T(8,128)S(1)} %bitcast.111, f32[512]{0:T(512)S(1)} %get-tuple-element.16, f32[512]{0:T(512)S(1)} %get-tuple-element.17), kind=kOutput, calls=%fused_computation.17 | convolution fusion | flops 1611399168 | bytes 2101248 | tf_op jit(solution)/shard_map/ax,tay->txy/dot_general | solution.py:109
  133.0 5.6 %fusion.2 = f32[1,512,512]{2,1,0:T(8,128)S(1)} fusion(f32[1,512,512]{2,1,0:T(8,128)S(1)} %copy-done, f32[512,512]{0,1:T(8,128)S(1)} %convolution_bitcast_fusion.3, f32[512]{0:T(512)S(1)} %get-tuple-element.16, f32[512]{0:T(512)S(1)} %get-tuple-element.17), kind=kOutput, calls=%fused_computation.20 | convolution fusion | flops 1611923456 | bytes 3149824 | tf_op jit(solution)/shard_map/txb,by->txy/dot_general | solution.py:110
  140.4 3.0 %collective-permute-done.2 = f32[1,512,512]{2,1,0:T(8,128)S(1)} collective-permute-done((f32[1,512,512]{2,1,0:T(8,128)S(1)}, f32[1,512,512]{2,1,0:T(8,128)S(1)}, u32[]{:S(2)}, u32[]{:S(2)}) %collective-permute-start.2) | collective-permute-done | bytes 1048608 | tf_op jit(solution)/shard_map/ppermute | solution.py:19
  143.4 4.1 %multiply_subtract_fusion.1 = (f32[1,512,512]{2,1,0:T(8,128)S(1)}, f32[1,512,512]{2,1,0:T(8,128)}, f32[1,512,512]{2,1,0:T(8,128)S(1)}) fusion(f32[1,512,512]{2,1,0:T(8,128)S(1)} %copy-done.5, f32[1,511,512]{2,1,0:T(8,128)S(1)} %slice_subtract_fusion.1, f32[1,512,512]{2,1,0:T(8,128)S(1)} %get-tuple-element.13, f32[1,512,511]{2,1,0:T(8,128)S(1)} %slice_subtract_fusion, ...), kind=kLoop, calls=%fused_computation.85 | loop fusion | flops 15990784 | bytes 11530241 | tf_op jit(solution)/shard_map/sub | solution.py:96
  149.0 14.2 %collective-permute-start.3 = (f32[1,512,512]{2,1,0:T(8,128)S(1)}, f32[1,512,512]{2,1,0:T(8,128)S(1)}, u32[]{:S(2)}, u32[]{:S(2)}) collective-permute-start(f32[1,512,512]{2,1,0:T(8,128)S(1)} %get-tuple-element.14), channel_id=1, source_target_pairs={{0,1},{1,2},{2,3},{3,4},{4,5},{5,6},{6,7},{7,8},{8,9},{9,10},{10,1... | collective-permute-start | bytes 3145736 | tf_op jit(solution)/shard_map/ppermute | solution.py:19
  163.3 2.0 collective-permute-done.3
  165.3 7.7 %convolution_bitcast_fusion.2 = f32[512,512]{0,1:T(8,128)S(1)} fusion(f32[1,512,512]{2,1,0:T(8,128)S(1)} %get-tuple-element.14, f32[1,512,512]{2,1,0:T(8,128)S(1)} %collective-permute-done.3, f32[512,512]{1,0:T(8,128)S(1)} %copy-done.7, f32[1,512,511]{2,1,0:T(8,128)S(1)} %bitcast.110, f32[1,512,512]{2,1,0:T(8,128)S(1)} %get-tuple-element.7, ...), kind=kOutput, calls=%fused_computation.14 | convolution fusion | flops 1613496320 | bytes 8389121 | tf_op jit(solution)/shard_map/ax,txy->tay/dot_general | solution.py:102
  173.0 7.4 %convolution_bitcast_fusion.1 = f32[1,512,512]{2,1,0:T(8,128)S(1)} fusion(f32[512,512]{0,1:T(8,128)S(1)} %convolution_bitcast_fusion.2, f32[512]{0:T(512)S(1)} %get-tuple-element.16, f32[512]{0:T(512)S(1)} %get-tuple-element.17), kind=kOutput, calls=%fused_computation.13 | convolution fusion | flops 1611399168 | bytes 2101248 | tf_op jit(solution)/shard_map/txy,by->txb/dot_general | solution.py:103
  181.4 40.4 %all_to_all.43 = f32[1,512,512]{2,0,1:T(1,128)S(1)} all-to-all(f32[1,512,512]{2,0,1:T(1,128)S(1)} %copy.22), channel_id=1, replica_groups=mesh['grp'=2,'tm'=16] {'tm'}, dimensions={1} | all-to-all | bytes 2097152 | tf_op jit(solution)/shard_map/all_to_all | solution.py:104
  221.9 1.6 add_divide_fusion.2
  225.3 29.8 %all_to_all.44 = f32[16,32,512]{2,1,0:T(8,128)S(1)} all-to-all(f32[16,32,512]{2,1,0:T(8,128)S(1)} %copy.25), channel_id=1, replica_groups=mesh['grp'=2,'tm'=16] {'tm'}, dimensions={0} | all-to-all | bytes 2097152 | tf_op jit(solution)/shard_map/all_to_all | solution.py:108
  255.1 5.6 %convolution_bitcast_fusion = f32[512,512]{0,1:T(8,128)S(1)} fusion(f32[512,512]{1,0:T(8,128)S(1)} %bitcast.112, f32[512]{0:T(512)S(1)} %get-tuple-element.16, f32[512]{0:T(512)S(1)} %get-tuple-element.17), kind=kOutput, calls=%fused_computation.12 | convolution fusion | flops 1611399168 | bytes 2101248 | tf_op jit(solution)/shard_map/ax,tay->txy/dot_general | solution.py:109
  260.6 6.6 %fusion.3 = f32[1,512,512]{2,1,0:T(8,128)} fusion(f32[1,512,512]{2,1,0:T(8,128)S(1)} %fusion.2, f32[512,512]{0,1:T(8,128)S(1)} %convolution_bitcast_fusion, f32[512]{0:T(512)S(1)} %get-tuple-element.16, f32[512]{0:T(512)S(1)} %get-tuple-element.17), kind=kOutput, calls=%fused_computation.21 | convolution fusion | flops 1611923456 | bytes 3149824 | tf_op jit(solution)/shard_map/txb,by->txy/dot_general | solution.py:110
  (41 shorter events, 14.5 us)
Async XLA Ops:
  0.6 4.9 %collective-permute-start = (f32[1,512,512]{2,1,0:T(8,128)}, f32[1,512,512]{2,1,0:T(8,128)}, u32[]{:S(2)}, u32[]{:S(2)}) collective-permute-start(f32[1,512,512]{2,1,0:T(8,128)} %param.9), channel_id=1, source_target_pairs={{1,0},{2,1},{3,2},{4,3},{5,4},{6,5},{7,6},{8,7},{9,8},{10,9},{11,1... | collective-permute-start | bytes 3145736 | tf_op jit(solution)/shard_map/ppermute | solution.py:19
  1.9 2.1 copy-start
  1.9 3.6 %copy-start.8 = (f32[1,512,512]{2,1,0:T(8,128)S(1)}, f32[1,512,512]{2,1,0:T(8,128)}, u32[]{:S(2)}) copy-start(f32[1,512,512]{2,1,0:T(8,128)} %param.7) | copy-start | bytes 3145732
  4.0 1.5 copy-start.1
  4.0 1.6 copy-start.2
  4.0 1.9 copy-start.3
  13.0 17.1 %collective-permute-start.1 = (f32[1,512,512]{2,1,0:T(8,128)}, f32[1,512,512]{2,1,0:T(8,128)}, u32[]{:S(2)}, u32[]{:S(2)}) collective-permute-start(f32[1,512,512]{2,1,0:T(8,128)} %get-tuple-element.15), channel_id=1, source_target_pairs={{0,1},{1,2},{2,3},{3,4},{4,5},{5,6},{6,7},{7,8},{8,9},{9,10},{10,1... | collective-permute-start | bytes 3145736 | tf_op jit(solution)/shard_map/ppermute | solution.py:19
  30.1 0.7 copy-start.9
  50.8 40.4 %all-to-all-start = ((f32[1,512,512]{2,0,1:T(1,128)}), f32[1,512,512]{2,0,1:T(1,128)}, u32[]{:S(2)}, u32[]{:S(2)}) async-start(f32[1,512,512]{2,0,1:T(1,128)} %copy.18), calls=%async_computation | async-start | bytes 2097152 | tf_op jit(solution)/shard_map/all_to_all | solution.py:104
  138.6 4.8 %collective-permute-start.2 = (f32[1,512,512]{2,1,0:T(8,128)S(1)}, f32[1,512,512]{2,1,0:T(8,128)S(1)}, u32[]{:S(2)}, u32[]{:S(2)}) collective-permute-start(f32[1,512,512]{2,1,0:T(8,128)S(1)} %fusion.2), channel_id=1, source_target_pairs={{1,0},{2,1},{3,2},{4,3},{5,4},{6,5},{7,6},{8,7},{9,8},{10,9},{11,1... | collective-permute-start | bytes 3145736 | tf_op jit(solution)/shard_map/ppermute | solution.py:19
  140.3 3.2 %copy-start.4 = (f32[512,512]{1,0:T(8,128)S(1)}, f32[512,512]{1,0:T(8,128)}, u32[]{:S(2)}) copy-start(f32[512,512]{1,0:T(8,128)} %param.11) | copy-start | bytes 3145732
  140.3 3.2 %copy-start.5 = (f32[1,512,512]{2,1,0:T(8,128)S(1)}, f32[1,512,512]{2,1,0:T(8,128)}, u32[]{:S(2)}) copy-start(f32[1,512,512]{2,1,0:T(8,128)} %get-tuple-element.10) | copy-start | bytes 3145732
  147.5 1.5 copy-start.6
  147.5 17.7 %copy-start.7 = (f32[512,512]{1,0:T(8,128)S(1)}, f32[512,512]{1,0:T(8,128)}, u32[]{:S(2)}) copy-start(f32[512,512]{1,0:T(8,128)} %param.10) | copy-start | bytes 3145732
  149.0 16.2 %collective-permute-start.3 = (f32[1,512,512]{2,1,0:T(8,128)S(1)}, f32[1,512,512]{2,1,0:T(8,128)S(1)}, u32[]{:S(2)}, u32[]{:S(2)}) collective-permute-start(f32[1,512,512]{2,1,0:T(8,128)S(1)} %get-tuple-element.14), channel_id=1, source_target_pairs={{0,1},{1,2},{2,3},{3,4},{4,5},{5,6},{6,7},{7,8},{8,9},{9,10},{10,1... | collective-permute-start | bytes 3145736 | tf_op jit(solution)/shard_map/ppermute | solution.py:19
where the time goes:
time: 271 us; the launch traced here: 267 us
  blocking collectives  102 us (38%)
  matrix products  61.7 us (23%)
  starting transfers between devices  49.9 us (18%)
  waiting for transfers between devices  30.4 us (11%)
  other arithmetic  15.5 us (6%)
  local copies, waits for them, and re-layouts  6.84 us (3%)
    all_to_all x2, blocking collectives, local(): lax.all_to_all(solved, 'tm', split_axis=0, concat_axis=1, tiled=True)  61.5 us
    all_to_all x1, blocking collectives, local(): lax.all_to_all(spectral, 'tm', split_axis=1, concat_axis=0, tiled=True)  40.4 us
    ppermute x4, starting transfers between devices, from_behind(): lax.ppermute(value, axis, [(source, source + steps) for source in range(f...  32.5 us
    all_to_all x1, waiting for transfers between devices, local(): lax.all_to_all(spectral, 'tm', split_axis=1, concat_axis=0, tiled=True)  22.7 us
    dot_general x2, matrix products, local(): spectral = jnp.einsum('ax,txy->tay', table_x, source, precision=highest)  18.1 us
    all_to_all x1, starting transfers between devices, local(): lax.all_to_all(spectral, 'tm', split_axis=1, concat_axis=0, tiled=True)  17.4 us
    dot_general x2, matrix products, local(): spectral = jnp.einsum('txy,by->txb', spectral, table_y, precision=highest)  15 us
    dot_general x2, matrix products, local(): field = jnp.einsum('txb,by->txy', field, table_y, precision=highest)  12.1 us
  transfers between devices with their start and end apart: 5, of which 5 were waited for; matrix products, arithmetic and copies ran while one was open for 1% of the time, Pallas kernels for 0%

commit v1 on v0

v1 whole, which is shorter than its diff:
```python
import functools

import jax
import jax.numpy as jnp
import ml_dtypes
import numpy as np
from jax import lax
from jax.experimental import pallas as pl
from jax.experimental.pallas import tpu as pltpu
from jax.sharding import PartitionSpec as P

NEWTON = 3

PRIMAL_STEP = 0.5
DUAL_STEP = 0.5
CONGESTION = 0.1
SCREENING = 0.05

CHUNKS = 4
TILE = 32
VMEM_BYTES = 56 * 1024 * 1024
F32 = jnp.float32
BF16 = jnp.bfloat16


def cosine_table(length):
    freq = np.arange(length, dtype=np.float64)[:, None]
    place = np.arange(length, dtype=np.float64)[None, :]
    scale = np.where(freq == 0, np.sqrt(1.0 / length), np.sqrt(2.0 / length))
    return scale * np.cos(np.pi * (place + 0.5) * freq / length)


def spectrum(length):
    return 2.0 - 2.0 * np.cos(np.pi * np.arange(length, dtype=np.float64) / length)


def halves(table):
    high = table.astype(np.float32).astype(ml_dtypes.bfloat16)
    low = (table - high.astype(np.float64)).astype(np.float32).astype(ml_dtypes.bfloat16)
    return np.stack([high, low])


def split(value):
    high = value.astype(BF16)
    return high, (value - high.astype(F32)).astype(BF16)


def product(a_high, a_low, b_high, b_low):
    dot = functools.partial(jnp.dot, preferred_element_type=F32)
    return dot(a_high, b_high) + (dot(a_low, b_high) + dot(a_high, b_low))


def two_sided(read, left, right, mid, write, rows):
    step = min(256, rows)
    for r0 in range(0, rows, step):
        high, low = split(read(r0, step))
        high, low = split(product(high, low, right[0], right[1]))
        mid[0, r0 : r0 + step, :] = high
        mid[1, r0 : r0 + step, :] = low
    for r0 in range(0, rows, step):
        here = slice(r0, r0 + step)
        write(r0, step, product(left[0, here, :], left[1, here, :], mid[0], mid[1]))


def proximal(density, flux_x, flux_y, time_grad, grad_x, grad_y, running_cost):
    moment_x = flux_x + PRIMAL_STEP * grad_x
    moment_y = flux_y + PRIMAL_STEP * grad_y
    kinetic = 0.5 * PRIMAL_STEP * (moment_x * moment_x + moment_y * moment_y)
    slope = 1.0 + CONGESTION * PRIMAL_STEP
    offset = density + PRIMAL_STEP * (time_grad - running_cost)
    root = jnp.exp2(jnp.log2(kinetic * (1.0 / slope)) * (1.0 / 3.0))
    guess = jnp.maximum(offset * (1.0 / slope), 0.0) + root
    for sweep in range(NEWTON):
        shifted = guess + PRIMAL_STEP
        linear = slope * guess - offset
        residue = linear * shifted * shifted - kinetic
        derivative = slope * shifted * shifted + 2.0 * linear * shifted
        guess = jnp.maximum(guess - residue / derivative, 0.0)
    weight = guess / (guess + PRIMAL_STEP)
    return (guess, weight * moment_x, weight * moment_y)


def forward_half(flag, fields, pot, following, cost, init, table_x, table_yt, outs, hat, work, mid):
    density, flux_x, flux_y = fields
    rows, cols = pot.shape
    first = flag[0] == 1
    last = flag[1] == 1

    def tile(index, carry):
        r0 = pl.multiple_of(index * TILE, TILE)
        here = pl.ds(r0, TILE)
        row = lax.broadcasted_iota(jnp.int32, (TILE, cols), 0)
        col = lax.broadcasted_iota(jnp.int32, (TILE, cols), 1)
        p = pot[here, :]
        below = pl.multiple_of(jnp.minimum(r0 + TILE, rows - 8), 8)
        edge = pot[pl.ds(below, 8), :][0:1, :]
        p_down = jnp.where(row == TILE - 1, edge, pltpu.roll(p, TILE - 1, 0))
        grad_x = jnp.where(row + r0 == rows - 1, 0.0, p_down - p)
        grad_y = jnp.where(col == cols - 1, 0.0, pltpu.roll(p, cols - 1, 1) - p)
        time_grad = jnp.where(last, 0.0, following[here, :] - p)
        old, old_x, old_y = density[here, :], flux_x[here, :], flux_y[here, :]
        new, new_x, new_y = proximal(old, old_x, old_y, time_grad, grad_x, grad_y, cost[here, :])
        outs[0][here, :] = new
        outs[1][here, :] = new_x
        outs[2][here, :] = new_y
        bar = 2.0 * new - old
        bar_x = 2.0 * new_x - old_x
        bar_y = jnp.where(col == cols - 1, 0.0, 2.0 * new_y - old_y)
        div_y = bar_y - jnp.where(col == 0, 0.0, pltpu.roll(bar_y, 1, 1))
        bar_x = jnp.where(row + r0 == rows - 1, 0.0, bar_x)
        before = jnp.where(row == 0, carry, pltpu.roll(bar_x, 1, 0))
        start = jnp.where(first, init[here, :], 0.0)
        work[1, here, :] = bar
        work[0, here, :] = bar - start + div_y + (bar_x - before)
        return bar_x[TILE - 1 : TILE, :]

    lax.fori_loop(0, rows // TILE, tile, jnp.zeros((1, cols), F32))

    for part in range(2):
        def read(r0, step):
            return work[part, r0 : r0 + step, :]

        def write(r0, step, value):
            hat[part, r0 : r0 + step, :] = value

        two_sided(read, table_x, table_yt, mid, write, rows)


def backward_half(modes, part, pot, table_xt, table_y, out, mid):
    def read(r0, step):
        return modes[part, r0 : r0 + step, :]

    def write(r0, step, value):
        here = slice(r0, r0 + step)
        out[here, :] = pot[here, :] + DUAL_STEP * value

    two_sided(read, table_xt, table_y, mid, write, pot.shape[0])


def first_kernel(flag, density, flux_x, flux_y, pot, following, cost, init, tx, tyt, o_d, o_x, o_y, hat, work, mid):
    forward_half(flag, (density, flux_x, flux_y), pot, following, cost, init, tx, tyt, (o_d, o_x, o_y), hat, work, mid)


def middle_kernel(
    flag, modes, density, flux_x, flux_y, pot, following, cost, init, tx, txt, ty, tyt,
    o_d, o_x, o_y, o_p, hat, work, mid, moved,
):
    backward_half(modes, 0, pot, txt, ty, o_p, mid)
    backward_half(modes, 1, following, txt, ty, moved, mid)
    forward_half(flag, (density, flux_x, flux_y), o_p, moved, cost, init, tx, tyt, (o_d, o_x, o_y), hat, work, mid)


def last_kernel(modes, pot, txt, ty, o_p, mid):
    backward_half(modes, 0, pot, txt, ty, o_p, mid)


def solve_kernel(
    n, wd, coef, other, x, wd_in, ab_out, ab_in, ab_own, p_in, p_out, q_in, q_out, give, got, own, x_out,
    core_s, core_r, y_s, y_r, p_s, p_r, q_s, q_r, ret_s, ret_r, x_s, x_r,
):
    me = lax.axis_index("tm")
    core = lax.rem(me, 2)
    side = lax.rem(me // 2, 2)
    g = me // 4
    groups = n // 4
    mate = me + 1 - 2 * core
    across = me + 2 - 4 * side
    ahead, behind = me + 4, me - 4
    half = wd.shape[1] // 2
    quarter = half // 2
    rows = quarter // CHUNKS
    cols = wd.shape[2]

    barrier = pltpu.get_barrier_semaphore()
    pl.semaphore_signal(barrier, inc=1, device_id={"tm": mate}, device_id_type=pl.DeviceIdType.MESH)
    pl.semaphore_signal(barrier, inc=1, device_id={"tm": across}, device_id_type=pl.DeviceIdType.MESH)

    @pl.when(g > 0)
    def _():
        pl.semaphore_signal(barrier, inc=1, device_id={"tm": behind}, device_id_type=pl.DeviceIdType.MESH)

    @pl.when(g < groups - 1)
    def _():
        pl.semaphore_signal(barrier, inc=1, device_id={"tm": ahead}, device_id_type=pl.DeviceIdType.MESH)

    @pl.when(g == 0)
    def _():
        p_in[...] = jnp.zeros_like(p_in)

    @pl.when(g == groups - 1)
    def _():
        q_in[...] = jnp.zeros_like(q_in)

    peers = 2 + (g > 0).astype(jnp.int32) + (g < groups - 1).astype(jnp.int32)
    pl.semaphore_wait(barrier, peers)

    def remote(src, dst, send, recv, target):
        return pltpu.make_async_remote_copy(
            src_ref=src, dst_ref=dst, send_sem=send, recv_sem=recv,
            device_id={"tm": target}, device_id_type=pl.DeviceIdType.MESH,
        )

    def at(k):
        return pl.ds(pl.multiple_of(k * rows, rows), rows)

    def in_half(k):
        part = jnp.where(k < CHUNKS, 1 - side, side)
        return pl.multiple_of(part * quarter + lax.rem(k, CHUNKS) * rows, rows)

    def core_copy(k):
        src = wd.at[:, pl.ds(pl.multiple_of((1 - core) * half + in_half(k), rows), rows), :]
        return remote(src, wd_in.at[:, pl.ds(in_half(k), rows), :], core_s.at[k], core_r.at[k], mate)

    def y_copy(k):
        return remote(ab_out.at[:, at(k), :], ab_in.at[:, at(k), :], y_s.at[k], y_r.at[k], across)

    def p_copy(k):
        return remote(p_out.at[at(k), :], p_in.at[at(k), :], p_s.at[k], p_r.at[k], ahead)

    def q_copy(k):
        return remote(q_out.at[at(k), :], q_in.at[at(k), :], q_s.at[k], q_r.at[k], behind)

    def ret_copy(part, k):
        return remote(give.at[part, at(k), :], got.at[part, at(k), :], ret_s.at[part, k], ret_r.at[part, k], across)

    def x_copy(k):
        here = pl.ds(in_half(k), rows)
        there = pl.ds(pl.multiple_of(core * half + in_half(k), rows), rows)
        return remote(x_out.at[:, here, :], x.at[:, there, :], x_s.at[k], x_r.at[k], mate)

    def loop(count, body):
        lax.fori_loop(0, count, lambda k, c: (body(k), c)[1], 0)

    loop(2 * CHUNKS, lambda k: core_copy(k).start())

    low = core == 0

    def sources(k):
        here = pl.ds(in_half(k), rows)
        mine = pl.ds(pl.multiple_of(core * half + in_half(k), rows), rows)
        w_a, d_a = wd[0, mine, :], wd[1, mine, :]
        w_b, d_b = wd_in[0, here, :], wd_in[1, here, :]
        w0 = jnp.where(low, w_a, w_b)
        s1 = jnp.where(low, w_b - d_a, w_a - d_b)
        d1 = jnp.where(low, d_b, d_a)
        return w0, s1, d1, [coef[j, here, :] for j in range(6)]

    def carries(k):
        w0, s1, d1, (f0, f1, h0, h1, h2, _) = sources(k)
        return f1 * (s1 + f0 * w0) - d1, h0 * (w0 + h1 * (s1 - h2 * d1))

    def out_chunk(k):
        core_copy(k).wait_recv()
        a, b = carries(k)
        ab_out[0, at(k), :] = a
        ab_out[1, at(k), :] = b
        y_copy(k).start()

    loop(CHUNKS, out_chunk)

    def own_chunk(k):
        core_copy(k + CHUNKS).wait_recv()
        a, b = carries(k + CHUNKS)
        ab_own[0, at(k), :] = a
        ab_own[1, at(k), :] = b

    loop(CHUNKS, own_chunk)

    left = side == 0

    def ordered(part, k, first, second):
        here = pl.ds(in_half(k + CHUNKS), rows)
        mine, theirs = ab_own[part, at(k), :], ab_in[part, at(k), :]
        rate, rate_other = coef[first, here, :] * coef[second, here, :], other[part, at(k), :]
        return (
            jnp.where(left, mine, theirs), jnp.where(left, rate, rate_other),
            jnp.where(left, theirs, mine), jnp.where(left, rate_other, rate),
        )

    def step(s):
        @pl.when(s < CHUNKS)
        def _():
            y_copy(s).wait_recv()

        kp = s - g

        @pl.when((kp >= 0) & (kp < CHUNKS))
        def _():
            @pl.when(g > 0)
            def _():
                p_copy(kp).wait_recv()

            a0, r0, a1, r1 = ordered(0, kp, 0, 1)
            enter = p_in[at(kp), :]
            middle = a0 + r0 * enter

            @pl.when(g < groups - 1)
            def _():
                p_out[at(kp), :] = a1 + r1 * middle
                p_copy(kp).start()

            own[0, at(kp), :] = jnp.where(left, enter, middle)
            give[0, at(kp), :] = jnp.where(left, middle, enter)
            ret_copy(0, kp).start()

        kq = s - (groups - 1 - g)

        @pl.when((kq >= 0) & (kq < CHUNKS))
        def _():
            @pl.when(g < groups - 1)
            def _():
                q_copy(kq).wait_recv()

            b0, r0, b1, r1 = ordered(1, kq, 2, 3)
            enter = q_in[at(kq), :]
            middle = b1 + r1 * enter

            @pl.when(g > 0)
            def _():
                q_out[at(kq), :] = b0 + r0 * middle
                q_copy(kq).start()

            own[1, at(kq), :] = jnp.where(left, middle, enter)
            give[1, at(kq), :] = jnp.where(left, enter, middle)
            ret_copy(1, kq).start()

    loop(CHUNKS + groups - 1, step)

    def finish(k, carry_p, carry_q):
        w0, s1, d1, (f0, f1, h0, h1, h2, g0) = sources(k)
        q2 = carry_q - h2 * d1
        q1 = h1 * (s1 + q2)
        x0 = (w0 + carry_p + q1) * g0
        x1 = h1 * x0 + q1
        x2 = h2 * x1 + q2
        here = pl.ds(in_half(k), rows)
        mine = pl.ds(pl.multiple_of(core * half + in_half(k), rows), rows)
        x[0, mine, :] = jnp.where(low, x0, x1)
        x[1, mine, :] = jnp.where(low, x1, x2)
        x_out[0, here, :] = jnp.where(low, x1, x0)
        x_out[1, here, :] = jnp.where(low, x2, x1)
        x_copy(k).start()

    loop(CHUNKS, lambda k: finish(k + CHUNKS, own[0, at(k), :], own[1, at(k), :]))

    def returned(k):
        ret_copy(0, k).wait_recv()
        ret_copy(1, k).wait_recv()
        finish(k, got[0, at(k), :], got[1, at(k), :])

    loop(CHUNKS, returned)

    def drain(k):
        core_copy(k).wait_send()
        x_copy(k).wait_send()
        x_copy(k).wait_recv()

    loop(2 * CHUNKS, drain)

    def drain_more(k):
        y_copy(k).wait_send()
        ret_copy(0, k).wait_send()
        ret_copy(1, k).wait_send()

        @pl.when(g < groups - 1)
        def _():
            p_copy(k).wait_send()

        @pl.when(g > 0)
        def _():
            q_copy(k).wait_send()

    loop(CHUNKS, drain_more)


def vmem(count):
    return [pl.BlockSpec(memory_space=pltpu.VMEM)] * count


def local_call(kernel, inputs, outs, scratch, flag=None):
    specs = vmem(len(inputs))
    if flag is not None:
        specs = [pl.BlockSpec(memory_space=pltpu.SMEM)] + specs
        inputs = [flag] + inputs
    return pl.pallas_call(
        kernel,
        out_shape=[jax.ShapeDtypeStruct(shape, F32) for shape in outs],
        in_specs=specs,
        out_specs=vmem(len(outs)),
        scratch_shapes=scratch,
        compiler_params=pltpu.CompilerParams(vmem_limit_bytes=VMEM_BYTES),
    )(*inputs)


def solve(n, wd, coef, other):
    _, rows, cols = wd.shape
    half, quarter = rows // 2, rows // 4
    dma = pltpu.SemaphoreType.DMA
    two = pltpu.VMEM((2, quarter, cols), F32)
    one = pltpu.VMEM((quarter, cols), F32)
    return pl.pallas_call(
        functools.partial(solve_kernel, n),
        out_shape=jax.ShapeDtypeStruct((2, rows, cols), F32),
        in_specs=vmem(3),
        out_specs=pl.BlockSpec(memory_space=pltpu.VMEM),
        scratch_shapes=[
            pltpu.VMEM((2, half, cols), F32), two, two, two, one, one, one, one, two, two, two,
            pltpu.VMEM((2, half, cols), F32),
            dma((2 * CHUNKS,)), dma((2 * CHUNKS,)), dma((CHUNKS,)), dma((CHUNKS,)),
            dma((CHUNKS,)), dma((CHUNKS,)), dma((CHUNKS,)), dma((CHUNKS,)),
            dma((2, CHUNKS)), dma((2, CHUNKS)), dma((2 * CHUNKS,)), dma((2 * CHUNKS,)),
        ],
        compiler_params=pltpu.CompilerParams(
            vmem_limit_bytes=VMEM_BYTES, collective_id=0, has_side_effects=True
        ),
    )(wd, coef, other)


def time_factors(n, position, rows, cols):
    lam_x = jnp.asarray(spectrum(rows), F32)
    lam_y = jnp.asarray(spectrum(cols), F32)
    half, quarter = rows // 2, rows // 4
    core, side, chip = position % 2, (position // 2) % 2, position // 2

    def pivots(start, count):
        mu = SCREENING + lax.dynamic_slice_in_dim(lam_x, start, count)[:, None] + lam_y[None, :]
        r = 2.0 / (mu + 2.0 + jnp.sqrt(mu * (mu + 4.0)))
        log_r = jnp.log(r)

        def inverse(i):
            power = jnp.exp(log_r * (2 * i + 1).astype(F32))
            return r * (1.0 + power) / (1.0 + power * r * r)

        return mu, inverse

    mu, inverse = pivots(core * half, half)
    i0 = 2 * chip
    h1 = inverse(n - 2 - i0)
    h2 = jnp.where(i0 + 2 == n, 0.0, inverse(jnp.maximum(n - 3 - i0, 0)))
    g0 = 1.0 / (mu + 2.0 - inverse(i0 - 1) - h1)
    coef = jnp.stack([inverse(i0), inverse(i0 + 1), inverse(n - 1 - i0), h1, h2, g0])
    _, inverse = pivots(core * half + side * quarter, quarter)
    j0 = 2 * (chip + 1 - 2 * side)
    other = jnp.stack([inverse(j0) * inverse(j0 + 1), inverse(n - 1 - j0) * inverse(n - 2 - j0)])
    return coef, other


def local(density, flux_x, flux_y, potential, initial_density, running_cost):
    n = lax.axis_size("tm")
    position = lax.axis_index("tm")
    _, rows, cols = density.shape
    shape = (rows, cols)
    following = lax.ppermute(potential[0], "tm", [(t, t - 1) for t in range(1, n)])
    coef, other = time_factors(n, position, rows, cols)
    flag = jnp.stack([position == 0, position == n - 1]).astype(jnp.int32)
    tx, ty = cosine_table(rows), cosine_table(cols)
    table_x, table_xt = jnp.asarray(halves(tx)), jnp.asarray(halves(tx.T))
    table_y, table_yt = jnp.asarray(halves(ty)), jnp.asarray(halves(ty.T))
    work = pltpu.VMEM((2, rows, cols), F32)
    mid = pltpu.VMEM((2, rows, cols), BF16)
    three = [shape] * 3
    hat_shape = (2, rows, cols)

    d, fx, fy, hat = local_call(
        first_kernel,
        [density[0], flux_x[0], flux_y[0], potential[0], following, running_cost, initial_density, table_x, table_yt],
        three + [hat_shape], [work, mid], flag,
    )
    modes = solve(n, hat, coef, other)
    d, fx, fy, pot, hat = local_call(
        middle_kernel,
        [modes, d, fx, fy, potential[0], following, running_cost, initial_density, table_x, table_xt, table_y, table_yt],
        three + [shape, hat_shape], [work, mid, pltpu.VMEM(shape, F32)], flag,
    )
    modes = solve(n, hat, coef, other)
    (pot,) = local_call(last_kernel, [modes, pot, table_xt, table_y], [shape], [mid])
    return (d[None], fx[None], fy[None], pot[None])


def solution(mesh):
    field = P(("grp", "tm"), None, None)
    flat = P("grp", None)
    return jax.shard_map(
        local,
        mesh=mesh,
        in_specs=(field, field, field, field, flat, flat),
        out_specs=(field, field, field, field),
        check_vma=False,
    )
```

time: 271 us -> 132 us (0.49); the launches traced: 267 us -> 132 us
  Pallas kernels: 0 us -> 119 us
  blocking collectives: 102 us -> 0 us
  matrix products: 61.7 us -> 0 us
  starting transfers between devices: 49.9 us -> 1.29 us
  waiting for transfers between devices: 30.4 us -> 0.01 us
  local copies, waits for them, and re-layouts: 6.84 us -> 1.01 us
  other arithmetic: 15.5 us -> 9.78 us
    pallas_call x0 -> x5, Pallas kernels: none -> 119 us  [the longest x2 80.5 us: solve(): pl.pallas_call(functools.partial(solve_kernel, n), out_shape=jax.ShapeDty...]
    all_to_all x3 -> x0, blocking collectives: 102 us -> none  [the longest x2 61.5 us: local(): lax.all_to_all(solved, 'tm', split_axis=0, concat_axis=1, tiled=True)]
    dot_general x12 -> x0, matrix products: 61.7 us -> none  [the longest x2 18.1 us: local(): spectral = jnp.einsum('ax,txy->tay', table_x, source, precision=highest)]
    ppermute x4 -> x1, starting transfers between devices: 32.5 us -> 1.29 us  [local(): lax.ppermute(potential[0], 'tm', [(t, t - 1) for t in range(1, n)])]
    all_to_all x1 -> x0, waiting for transfers between devices: 22.7 us -> none  [local(): lax.all_to_all(spectral, 'tm', split_axis=1, concat_axis=0, tiled=True)]
    all_to_all x1 -> x0, starting transfers between devices: 17.4 us -> none  [local(): lax.all_to_all(spectral, 'tm', split_axis=1, concat_axis=0, tiled=True)]
    sub x9 -> x0, other arithmetic: 15.4 us -> none  [the longest x2 9.36 us: local(): bar_x = 2.0 * new_x - flux_x]
    ppermute x4 -> x1, waiting for transfers between devices: 7.67 us -> 0.01 us  [local(): lax.ppermute(potential[0], 'tm', [(t, t - 1) for t in range(1, n)])]
  transfers between devices with their start and end apart: 5 -> 1, of which waited for: 5 -> 0; matrix products, arithmetic and copies ran while one was open for 1% -> 7% of each run, Pallas kernels for 0% -> 0%
where the time goes in v1:
time: 132 us
  Pallas kernels  119 us (90%)
  other arithmetic  9.78 us (7%)
    pallas_call x2, Pallas kernels, solve(): pl.pallas_call(functools.partial(solve_kernel, n), out_shape=jax.ShapeDty...  80.5 us
    pallas_call x3, Pallas kernels, local_call(): pl.pallas_call(kernel, out_shape=[jax.ShapeDtypeStruct(shape, F32) for sh...  38.5 us
    unnamed x5, other arithmetic  4.69 us
  transfers between devices with their start and end apart: 1, of which 0 were waited for; matrix products, arithmetic and copies ran while one was open for 7% of the time, Pallas kernels for 0%

profile of v1, /device:TPU:0, one launch (start us, length us, event | category | flops | bytes accessed | tf_op | source)
XLA Modules:
  0.0 131.9 jit_solution(16957525175918726976)
XLA Ops:
  0.6 0.0 copy-start.2
  0.6 1.3 collective-permute-start
  2.0 0.8 dynamic-slice_add_fusion.1
  2.8 0.8 dynamic-slice_add_fusion
  3.5 1.2 fusion.8
  4.8 1.2 fusion.11
  6.0 1.2 fusion.14
  7.2 1.3 fusion.26
  8.5 0.7 add_convert_fusion.flag
  9.1 0.8 pad_maximum_fusion.other
  9.9 0.0 copy-done.2
  9.9 0.5 fusion.43
  10.5 0.5 fusion.20
  11.0 0.8 fusion.5.coef
  11.9 0.0 copy-start
  11.9 0.0 collective-permute-done.following
  11.9 0.0 copy-start.1
  11.9 1.0 copy-done.1
  12.9 14.4 %shard_map.147 = (f32[512,512]{1,0:T(8,128)}, f32[512,512]{1,0:T(8,128)}, f32[512,512]{1,0:T(8,128)}, f32[2,512,512]{2,1,0:T(8,128)}) custom-call(s32[2]{0:T(128)} %add_convert_fusion.flag, f32[512,512]{1,0:T(8,128)} %bitcast.13, f32[512,512]{1,0:T(8,128)} %bitcast.14, f32[512,512]{1,0:T(8,128)} %bitcast.15, f32[512,512]{1,0:T(8,128)} %bitcast.11, ...), custom_call_target="tpu_custom_call" | custom-call | tf_op jit(solution)/shard_map/pallas_call | solution.py:385
  27.3 0.0 copy-done
  27.3 43.3 %shard_map.148.modes = f32[2,512,512]{2,1,0:T(8,128)} custom-call(f32[2,512,512]{2,1,0:T(8,128)} %get-tuple-element.13.wd, f32[6,256,512]{2,1,0:T(8,128)} %copy-done, f32[2,128,512]{2,1,0:T(8,128)} %pad_maximum_fusion.other), custom_call_target="tpu_custom_call" | custom-call | tf_op jit(solution)/shard_map/pallas_call | solution.py:401
  70.6 18.8 %shard_map.149 = (f32[512,512]{1,0:T(8,128)}, f32[512,512]{1,0:T(8,128)}, f32[512,512]{1,0:T(8,128)}, f32[512,512]{1,0:T(8,128)}, f32[2,512,512]{2,1,0:T(8,128)}) custom-call(s32[2]{0:T(128)} %add_convert_fusion.flag, f32[2,512,512]{2,1,0:T(8,128)} %shard_map.148.modes, f32[512,512]{1,0:T(8,128)} %get-tuple-element.14.density, ...), custom_call_target="tpu_custom_call" | custom-call | tf_op jit(solution)/shard_map/pallas_call | solution.py:385
  89.4 37.2 %shard_map.150.modes = f32[2,512,512]{2,1,0:T(8,128)} custom-call(f32[2,512,512]{2,1,0:T(8,128)} %get-tuple-element.20.wd, f32[6,256,512]{2,1,0:T(8,128)} %copy-done, f32[2,128,512]{2,1,0:T(8,128)} %pad_maximum_fusion.other), custom_call_target="tpu_custom_call" | custom-call | tf_op jit(solution)/shard_map/pallas_call | solution.py:401
  126.6 5.3 %shard_map.151 = f32[512,512]{1,0:T(8,128)} custom-call(f32[2,512,512]{2,1,0:T(8,128)} %shard_map.150.modes, f32[512,512]{1,0:T(8,128)} %get-tuple-element.21.pot, bf16[2,512,512]{2,1,0:T(8,128)(2,1)} %constant.76.clone.tyt.txt, bf16[2,512,512]{2,1,0:T(8,128)(2,1)} %constant.75.clone.tx.ty), custom_call_target="tpu_custom_call" | custom-call | tf_op jit(solution)/shard_map/pallas_call | solution.py:385
Async XLA Ops:
  0.6 9.3 %copy-start.2 = (f32[512]{0:T(512)S(1)}, f32[512]{0:T(512)}, u32[]{:S(2)}) copy-start(f32[512]{0:T(512)} %constant.74.clone) | copy-start | bytes 6148
  0.6 11.2 %collective-permute-start = (f32[512,512]{1,0:T(8,128)}, f32[512,512]{1,0:T(8,128)S(1)}, u32[]{:S(2)}, u32[]{:S(2)}) collective-permute-start(f32[512,512]{1,0:T(8,128)} %bitcast.10), channel_id=1, source_target_pairs={{1,0},{2,1},{3,2},{4,3},{5,4},{6,5},{7,6},{8,7},{9,8},{10,9},{11,1... | collective-permute-start | bytes 3145736 | tf_op jit(solution)/shard_map/ppermute | solution.py:453
  11.9 15.4 %copy-start = (f32[6,256,512]{2,1,0:T(8,128)}, f32[6,256,512]{2,1,0:T(8,128)S(1)}, u32[]{:S(2)}) copy-start(f32[6,256,512]{2,1,0:T(8,128)S(1)} %fusion.5.coef) | copy-start | bytes 9437188
  11.9 1.0 copy-start.1

commit v2 on v1

--- a/solution.py
+++ b/solution.py
@@ -17,8 +17,8 @@
 SCREENING = 0.05
 
 CHUNKS = 4
-TILE = 32
-VMEM_BYTES = 56 * 1024 * 1024
+TILE = 64
+VMEM_BYTES = 26 * 1024 * 1024
 F32 = jnp.float32
 BF16 = jnp.bfloat16
 
@@ -48,6 +48,11 @@
 def product(a_high, a_low, b_high, b_low):
     dot = functools.partial(jnp.dot, preferred_element_type=F32)
     return dot(a_high, b_high) + (dot(a_low, b_high) + dot(a_high, b_low))
+
+
+def inverse_of(value):
+    rough = pl.reciprocal(value, approx=True)
+    return rough * (2.0 - value * rough)
 
 
 def two_sided(read, left, right, mid, write, rows):
@@ -75,8 +80,8 @@
         linear = slope * guess - offset
         residue = linear * shifted * shifted - kinetic
         derivative = slope * shifted * shifted + 2.0 * linear * shifted
-        guess = jnp.maximum(guess - residue / derivative, 0.0)
-    weight = guess / (guess + PRIMAL_STEP)
+        guess = jnp.maximum(guess - residue * inverse_of(derivative), 0.0)
+    weight = guess * inverse_of(guess + PRIMAL_STEP)
     return (guess, weight * moment_x, weight * moment_y)
 
 

time: 132 us -> 112 us (0.85)
  Pallas kernels: 119 us -> 98.3 us
  local copies, waits for them, and re-layouts: 1.01 us -> 2.48 us
    pallas_call x3, Pallas kernels: 38.5 us -> 24.4 us  [local_call(): pl.pallas_call(kernel, out_shape=[jax.ShapeDtypeStruct(shape, F32) for sh...]
    pallas_call x2, Pallas kernels: 80.5 us -> 73.9 us  [solve(): pl.pallas_call(functools.partial(solve_kernel, n), out_shape=jax.ShapeDty...]
    unnamed x6 -> x18, local copies, waits for them, and re-layouts: 1.01 us -> 2.48 us
  transfers between devices with their start and end apart: 1 -> 1, of which waited for: 0 -> 0; matrix products, arithmetic and copies ran while one was open for 7% -> 8% of each run, Pallas kernels for 0% -> 0%
where the time goes in v2:
time: 112 us
  Pallas kernels  98.3 us (88%)
  other arithmetic  9.06 us (8%)
  local copies, waits for them, and re-layouts  2.48 us (2%)
  starting transfers between devices  1.29 us (1%)
    pallas_call x2, Pallas kernels, solve(): pl.pallas_call(functools.partial(solve_kernel, n), out_shape=jax.ShapeDty...  73.9 us
    pallas_call x3, Pallas kernels, local_call(): pl.pallas_call(kernel, out_shape=[jax.ShapeDtypeStruct(shape, F32) for sh...  24.4 us
    unnamed x5, other arithmetic  5.33 us
    unnamed x18, local copies, waits for them, and re-layouts  2.48 us
  transfers between devices with their start and end apart: 1, of which 0 were waited for; matrix products, arithmetic and copies ran while one was open for 8% of the time, Pallas kernels for 0%

profile of v2, /device:TPU:0, one launch (start us, length us, event | category | flops | bytes accessed | tf_op | source)
XLA Modules:
  0.0 112.0 jit_solution(9395492103308993692)
XLA Ops:
  0.6 0.0 copy-start.8
  0.6 1.3 %collective-permute-start = (f32[512,512]{1,0:T(8,128)}, f32[512,512]{1,0:T(8,128)S(1)}, u32[]{:S(2)}, u32[]{:S(2)}) collective-permute-start(f32[512,512]{1,0:T(8,128)} %bitcast.10), channel_id=1, source_target_pairs={{1,0},{2,1},{3,2},{4,3},{5,4},{6,5},{7,6},{8,7},{9,8},{10,9},{11,1... | collective-permute-start | bytes 3145736 | tf_op jit(solution)/shard_map/ppermute | solution.py:458
  2.0 0.8 dynamic-slice_add_fusion.1
  2.8 0.8 dynamic-slice_add_fusion
  3.6 0.0 copy-start.4
  3.6 0.0 copy-start.5
  3.6 1.4 %fusion.8 = f32[6,256,512]{2,1,0:T(8,128)S(1)} fusion(f32[]{:T(128)S(6)} %convert_element_type.34, f32[512]{0:T(512)} %constant.74.clone, f32[256]{0:T(256)S(1)} %dynamic-slice_add_fusion), kind=kLoop, calls=%fused_computation.17 | loop fusion | flops 1703935 | bytes 527364
  4.9 1.7 %fusion.11 = f32[6,256,512]{2,1,0:T(8,128)S(1)} fusion(f32[6,256,512]{2,1,0:T(8,128)S(1)} %fusion.8, f32[]{:T(128)S(6)} %convert_element_type.35, f32[512]{0:T(512)} %constant.74.clone, f32[256]{0:T(256)S(1)} %dynamic-slice_add_fusion), kind=kLoop, calls=%fused_computation.20 | loop fusion | flops 1703936 | bytes 527364
  6.6 1.2 %fusion.14 = f32[6,256,512]{2,1,0:T(8,128)S(1)} fusion(f32[6,256,512]{2,1,0:T(8,128)S(1)} %fusion.11, f32[]{:T(128)S(6)} %convert_element_type.36, f32[512]{0:T(512)} %constant.74.clone, f32[256]{0:T(256)S(1)} %dynamic-slice_add_fusion), kind=kLoop, calls=%fused_computation.23 | loop fusion | flops 1703936 | bytes 527364
  7.9 1.3 %fusion.26 = (f32[1,128,512]{2,1,0:T(8,128)S(1)}, f32[1,128,512]{2,1,0:T(8,128)S(1)}) fusion(f32[]{:T(128)S(6)} %convert_element_type.41, f32[]{:T(128)S(6)} %convert_element_type.40, f32[512]{0:T(512)} %constant.74.clone, f32[128]{0:T(128)S(1)} %dynamic-slice_add_fusion.1, f32[]{:T(128)S(6)} %convert_element_type.43, f32[]{:T(128)S(6)} %convert_element_type.42), kind=kLoop, calls=%fused_computation.43 | loop fusion | flops 2359296 | bytes 526864 | tf_op jit(solution)/shard_map/mul | solution.py:449
  9.1 0.1 add_convert_fusion.flag
  9.3 0.0 copy-done.8
  9.3 0.5 fusion.43
  9.8 0.5 fusion.20
  10.4 0.8 fusion.5.coef
  11.2 0.0 collective-permute-done.following
  11.3 0.0 copy-start.6
  11.3 1.2 %copy-done.6 = f32[1,512,512]{2,1,0:T(8,128)S(1)} copy-done((f32[1,512,512]{2,1,0:T(8,128)S(1)}, f32[1,512,512]{2,1,0:T(8,128)}, u32[]{:S(2)}) %copy-start.6) | copy-done | bytes 1048600
  12.5 1.2 %copy-done.7 = f32[1,512,512]{2,1,0:T(8,128)S(1)} copy-done((f32[1,512,512]{2,1,0:T(8,128)S(1)}, f32[1,512,512]{2,1,0:T(8,128)}, u32[]{:S(2)}) %copy-start.7) | copy-done | bytes 1048600
  13.7 9.0 %shard_map.147 = (f32[512,512]{1,0:T(8,128)S(1)}, f32[512,512]{1,0:T(8,128)S(1)}, f32[512,512]{1,0:T(8,128)S(1)}, f32[2,512,512]{2,1,0:T(8,128)S(1)}) custom-call(s32[2]{0:T(128)S(1)} %add_convert_fusion.flag, f32[512,512]{1,0:T(8,128)S(1)} %bitcast.13, f32[512,512]{1,0:T(8,128)S(1)} %bitcast.14, f32[512,512]{1,0:T(8,128)S(1)} %bitcast.15, ...), custom_call_target="tpu_custom_call" | custom-call | tf_op jit(solution)/shard_map/pallas_call | solution.py:390
  22.7 40.5 %shard_map.148.modes = f32[2,512,512]{2,1,0:T(8,128)S(1)} custom-call(f32[2,512,512]{2,1,0:T(8,128)S(1)} %get-tuple-element.13.wd, f32[6,256,512]{2,1,0:T(8,128)S(1)} %fusion.5.coef, f32[2,128,512]{2,1,0:T(8,128)S(1)} %pad_maximum_fusion.other), custom_call_target="tpu_custom_call" | custom-call | tf_op jit(solution)/shard_map/pallas_call | solution.py:406
  63.2 12.6 %shard_map.149 = (f32[512,512]{1,0:T(8,128)}, f32[512,512]{1,0:T(8,128)}, f32[512,512]{1,0:T(8,128)}, f32[512,512]{1,0:T(8,128)S(1)}, f32[2,512,512]{2,1,0:T(8,128)S(1)}) custom-call(s32[2]{0:T(128)S(1)} %add_convert_fusion.flag, f32[2,512,512]{2,1,0:T(8,128)S(1)} %shard_map.148.modes, f32[512,512]{1,0:T(8,128)S(1)} %get-tuple-element.14.density, ...), custom_call_target="tpu_custom_call" | custom-call | tf_op jit(solution)/shard_map/pallas_call | solution.py:390
  75.8 33.4 %shard_map.150.modes = f32[2,512,512]{2,1,0:T(8,128)S(1)} custom-call(f32[2,512,512]{2,1,0:T(8,128)S(1)} %get-tuple-element.20.wd, f32[6,256,512]{2,1,0:T(8,128)S(1)} %fusion.5.coef, f32[2,128,512]{2,1,0:T(8,128)S(1)} %pad_maximum_fusion.other), custom_call_target="tpu_custom_call" | custom-call | tf_op jit(solution)/shard_map/pallas_call | solution.py:406
  109.2 2.9 %shard_map.151 = f32[512,512]{1,0:T(8,128)} custom-call(f32[2,512,512]{2,1,0:T(8,128)S(1)} %shard_map.150.modes, f32[512,512]{1,0:T(8,128)S(1)} %get-tuple-element.21.pot, bf16[2,512,512]{2,1,0:T(8,128)(2,1)S(1)} %copy-done, bf16[2,512,512]{2,1,0:T(8,128)(2,1)S(1)} %copy-done.1), custom_call_target="tpu_custom_call" | custom-call | tf_op jit(solution)/shard_map/pallas_call | solution.py:390
  (12 shorter events, 0.1 us)
Async XLA Ops:
  0.6 8.6 %copy-start.8 = (f32[512]{0:T(512)S(1)}, f32[512]{0:T(512)}, u32[]{:S(2)}) copy-start(f32[512]{0:T(512)} %constant.74.clone) | copy-start | bytes 6148
  0.6 10.5 %collective-permute-start = (f32[512,512]{1,0:T(8,128)}, f32[512,512]{1,0:T(8,128)S(1)}, u32[]{:S(2)}, u32[]{:S(2)}) collective-permute-start(f32[512,512]{1,0:T(8,128)} %bitcast.10), channel_id=1, source_target_pairs={{1,0},{2,1},{3,2},{4,3},{5,4},{6,5},{7,6},{8,7},{9,8},{10,9},{11,1... | collective-permute-start | bytes 3145736 | tf_op jit(solution)/shard_map/ppermute | solution.py:458
  3.5 7.7 %copy-start = (bf16[2,512,512]{2,1,0:T(8,128)(2,1)S(1)}, bf16[2,512,512]{2,1,0:T(8,128)(2,1)}, u32[]{:S(2)}) copy-start(bf16[2,512,512]{2,1,0:T(8,128)(2,1)} %constant.76.clone.tyt.txt) | copy-start | bytes 3145732
  3.5 7.7 %copy-start.1 = (bf16[2,512,512]{2,1,0:T(8,128)(2,1)S(1)}, bf16[2,512,512]{2,1,0:T(8,128)(2,1)}, u32[]{:S(2)}) copy-start(bf16[2,512,512]{2,1,0:T(8,128)(2,1)} %constant.75.clone.tx.ty) | copy-start | bytes 3145732
  3.5 7.7 %copy-start.2 = (f32[1,512,512]{2,1,0:T(8,128)S(1)}, f32[1,512,512]{2,1,0:T(8,128)}, u32[]{:S(2)}) copy-start(f32[1,512,512]{2,1,0:T(8,128)} %param.15) | copy-start | bytes 3145732
  3.5 7.7 %copy-start.3 = (f32[512,512]{1,0:T(8,128)S(1)}, f32[512,512]{1,0:T(8,128)}, u32[]{:S(2)}) copy-start(f32[512,512]{1,0:T(8,128)} %cost.3) | copy-start | bytes 3145732
  3.6 7.7 %copy-start.4 = (f32[512,512]{1,0:T(8,128)S(1)}, f32[512,512]{1,0:T(8,128)}, u32[]{:S(2)}) copy-start(f32[512,512]{1,0:T(8,128)} %init.3) | copy-start | bytes 3145732
  3.6 7.7 %copy-start.5 = (f32[1,512,512]{2,1,0:T(8,128)S(1)}, f32[1,512,512]{2,1,0:T(8,128)}, u32[]{:S(2)}) copy-start(f32[1,512,512]{2,1,0:T(8,128)} %param.12) | copy-start | bytes 3145732
  11.3 1.2 %copy-start.6 = (f32[1,512,512]{2,1,0:T(8,128)S(1)}, f32[1,512,512]{2,1,0:T(8,128)}, u32[]{:S(2)}) copy-start(f32[1,512,512]{2,1,0:T(8,128)} %param.13) | copy-start | bytes 3145732
  12.5 1.2 %copy-start.7 = (f32[1,512,512]{2,1,0:T(8,128)S(1)}, f32[1,512,512]{2,1,0:T(8,128)}, u32[]{:S(2)}) copy-start(f32[1,512,512]{2,1,0:T(8,128)} %param.14) | copy-start | bytes 3145732

commit v3 on v2

--- a/solution.py
+++ b/solution.py
@@ -85,13 +85,13 @@
     return (guess, weight * moment_x, weight * moment_y)
 
 
-def forward_half(flag, fields, pot, following, cost, init, table_x, table_yt, outs, hat, work, mid):
+def forward_half(first, last, fields, pot, following, cost, init, table_x, table_yt, outs, hat, work, mid, ready=None):
     density, flux_x, flux_y = fields
     rows, cols = pot.shape
-    first = flag[0] == 1
-    last = flag[1] == 1
 
     def tile(index, carry):
+        if ready is not None:
+            ready(index)
         r0 = pl.multiple_of(index * TILE, TILE)
         here = pl.ds(r0, TILE)
         row = lax.broadcasted_iota(jnp.int32, (TILE, cols), 0)
@@ -142,8 +142,97 @@
     two_sided(read, table_xt, table_y, mid, write, pot.shape[0])
 
 
-def first_kernel(flag, density, flux_x, flux_y, pot, following, cost, init, tx, tyt, o_d, o_x, o_y, hat, work, mid):
-    forward_half(flag, (density, flux_x, flux_y), pot, following, cost, init, tx, tyt, (o_d, o_x, o_y), hat, work, mid)
+def factors(n, me, mu_ref, coef, other):
+    half, cols = coef.shape[1:]
+    quarter = half // 2
+    core, side, chip = lax.rem(me, 2), lax.rem(me // 2, 2), me // 2
+    ends = chip == n // 2 - 1
+
+    def roots(row):
+        mu = mu_ref[pl.ds(pl.multiple_of(row, TILE), TILE), :]
+        r = 2.0 / (mu + 2.0 + jnp.sqrt(mu * (mu + 4.0)))
+        return mu, r, r * r, jnp.log(r)
+
+    def three(i, r, r2, log_r):
+        power = jnp.exp(log_r * (2 * i + 1).astype(F32))
+        terms = []
+        for _ in range(4):
+            terms.append(1.0 + power)
+            power = power * r2
+        return [r * terms[j] / terms[j + 1] for j in range(3)]
+
+    def main(k, c):
+        mu, r, r2, log_r = roots(core * half + k * TILE)
+        here = pl.ds(pl.multiple_of(k * TILE, TILE), TILE)
+        before, f0, f1 = three(2 * chip - 1, r, r2, log_r)
+        h2, h1, h0 = three(n - 3 - 2 * chip, r, r2, log_r)
+        g0 = 1.0 / (mu + 2.0 - before - h1)
+        for j, value in enumerate((f0, f1, h0, h1, jnp.where(ends, 0.0, h2), g0)):
+            coef[j, here, :] = value
+        return c
+
+    lax.fori_loop(0, half // TILE, main, 0)
+
+    def rest(k, c):
+        _, r, r2, log_r = roots(core * half + side * quarter + k * TILE)
+        here = pl.ds(pl.multiple_of(k * TILE, TILE), TILE)
+        j0 = 2 * (chip + 1 - 2 * side)
+        for part, i in enumerate((j0, n - 2 - j0)):
+            one, two, _ = three(i, r, r2, log_r)
+            other[part, here, :] = one * two
+        return c
+
+    lax.fori_loop(0, quarter // TILE, rest, 0)
+
+
+def first_kernel(
+    n, density, flux_x, flux_y, pot, cost, init, tx, tyt, mu,
+    o_d, o_x, o_y, hat, following, coef, other, work, mid, send, recv,
+):
+    me = lax.axis_index("tm")
+    chunks = pot.shape[0] // TILE
+    barrier = pltpu.get_barrier_semaphore()
+
+    @pl.when(me > 0)
+    def _():
+        pl.semaphore_signal(barrier, inc=1, device_id={"tm": me - 1}, device_id_type=pl.DeviceIdType.MESH)
+
+    @pl.when(me < n - 1)
+    def _():
+        pl.semaphore_signal(barrier, inc=1, device_id={"tm": me + 1}, device_id_type=pl.DeviceIdType.MESH)
+
+    @pl.when(me == n - 1)
+    def _():
+        following[...] = jnp.zeros_like(following)
+
+    pl.semaphore_wait(barrier, (me > 0).astype(jnp.int32) + (me < n - 1).astype(jnp.int32))
+
+    def copy(k):
+        here = pl.ds(pl.multiple_of(k * TILE, TILE), TILE)
+        return pltpu.make_async_remote_copy(
+            src_ref=pot.at[here, :], dst_ref=following.at[here, :], send_sem=send.at[k], recv_sem=recv.at[k],
+            device_id={"tm": me - 1}, device_id_type=pl.DeviceIdType.MESH,
+        )
+
+    @pl.when(me > 0)
+    def _():
+        lax.fori_loop(0, chunks, lambda k, c: (copy(k).start(), c)[1], 0)
+
+    factors(n, me, mu, coef, other)
+
+    def ready(k):
+        @pl.when(me < n - 1)
+        def _():
+            copy(k).wait_recv()
+
+    forward_half(
+        me == 0, me == n - 1, (density, flux_x, flux_y), pot, following, cost, init, tx, tyt,
+        (o_d, o_x, o_y), hat, work, mid, ready,
+    )
+
+    @pl.when(me > 0)
+    def _():
+        lax.fori_loop(0, chunks, lambda k, c: (copy(k).wait_send(), c)[1], 0)
 
 
 def middle_kernel(
@@ -152,7 +241,8 @@
 ):
     backward_half(modes, 0, pot, txt, ty, o_p, mid)
     backward_half(modes, 1, following, txt, ty, moved, mid)
-    forward_half(flag, (density, flux_x, flux_y), o_p, moved, cost, init, tx, tyt, (o_d, o_x, o_y), hat, work, mid)
+    first, last = flag[0] == 1, flag[1] == 1
+    forward_half(first, last, (density, flux_x, flux_y), o_p, moved, cost, init, tx, tyt, (o_d, o_x, o_y), hat, work, mid)
 
 
 def last_kernel(modes, pot, txt, ty, o_p, mid):
@@ -382,18 +472,21 @@
     return [pl.BlockSpec(memory_space=pltpu.VMEM)] * count
 
 
-def local_call(kernel, inputs, outs, scratch, flag=None):
+def local_call(kernel, inputs, outs, scratch, flag=None, collective=None):
     specs = vmem(len(inputs))
     if flag is not None:
         specs = [pl.BlockSpec(memory_space=pltpu.SMEM)] + specs
         inputs = [flag] + inputs
+    params = dict(vmem_limit_bytes=VMEM_BYTES)
+    if collective is not None:
+        params.update(collective_id=collective, has_side_effects=True)
     return pl.pallas_call(
         kernel,
         out_shape=[jax.ShapeDtypeStruct(shape, F32) for shape in outs],
         in_specs=specs,
         out_specs=vmem(len(outs)),
         scratch_shapes=scratch,
-        compiler_params=pltpu.CompilerParams(vmem_limit_bytes=VMEM_BYTES),
+        compiler_params=pltpu.CompilerParams(**params),
     )(*inputs)
 
 
@@ -421,42 +514,13 @@
     )(wd, coef, other)
 
 
-def time_factors(n, position, rows, cols):
-    lam_x = jnp.asarray(spectrum(rows), F32)
-    lam_y = jnp.asarray(spectrum(cols), F32)
-    half, quarter = rows // 2, rows // 4
-    core, side, chip = position % 2, (position // 2) % 2, position // 2
-
-    def pivots(start, count):
-        mu = SCREENING + lax.dynamic_slice_in_dim(lam_x, start, count)[:, None] + lam_y[None, :]
-        r = 2.0 / (mu + 2.0 + jnp.sqrt(mu * (mu + 4.0)))
-        log_r = jnp.log(r)
-
-        def inverse(i):
-            power = jnp.exp(log_r * (2 * i + 1).astype(F32))
-            return r * (1.0 + power) / (1.0 + power * r * r)
-
-        return mu, inverse
-
-    mu, inverse = pivots(core * half, half)
-    i0 = 2 * chip
-    h1 = inverse(n - 2 - i0)
-    h2 = jnp.where(i0 + 2 == n, 0.0, inverse(jnp.maximum(n - 3 - i0, 0)))
-    g0 = 1.0 / (mu + 2.0 - inverse(i0 - 1) - h1)
-    coef = jnp.stack([inverse(i0), inverse(i0 + 1), inverse(n - 1 - i0), h1, h2, g0])
-    _, inverse = pivots(core * half + side * quarter, quarter)
-    j0 = 2 * (chip + 1 - 2 * side)
-    other = jnp.stack([inverse(j0) * inverse(j0 + 1), inverse(n - 1 - j0) * inverse(n - 2 - j0)])
-    return coef, other
-
-
 def local(density, flux_x, flux_y, potential, initial_density, running_cost):
     n = lax.axis_size("tm")
     position = lax.axis_index("tm")
     _, rows, cols = density.shape
     shape = (rows, cols)
-    following = lax.ppermute(potential[0], "tm", [(t, t - 1) for t in range(1, n)])
-    coef, other = time_factors(n, position, rows, cols)
+    mu = jnp.asarray(SCREENING + spectrum(rows)[:, None] + spectrum(cols)[None, :], F32)
+    dma = pltpu.SemaphoreType.DMA((rows // TILE,))
     flag = jnp.stack([position == 0, position == n - 1]).astype(jnp.int32)
     tx, ty = cosine_table(rows), cosine_table(cols)
     table_x, table_xt = jnp.asarray(halves(tx)), jnp.asarray(halves(tx.T))
@@ -466,10 +530,11 @@
     three = [shape] * 3
     hat_shape = (2, rows, cols)
 
-    d, fx, fy, hat = local_call(
-        first_kernel,
-        [density[0], flux_x[0], flux_y[0], potential[0], following, running_cost, initial_density, table_x, table_yt],
-        three + [hat_shape], [work, mid], flag,
+    d, fx, fy, hat, following, coef, other = local_call(
+        functools.partial(first_kernel, n),
+        [density[0], flux_x[0], flux_y[0], potential[0], running_cost, initial_density, table_x, table_yt, mu],
+        three + [hat_shape, shape, (6, rows // 2, cols), (2, rows // 4, cols)],
+        [work, mid, dma, dma], collective=1,
     )
     modes = solve(n, hat, coef, other)
     d, fx, fy, pot, hat = local_call(

time: 112 us -> 114 us (1.018)
  other arithmetic: 9.06 us -> 0.08 us
  local copies, waits for them, and re-layouts: 2.48 us -> 11.1 us
  Pallas kernels: 98.3 us -> 102 us
  starting transfers between devices: 1.29 us -> 0 us
    unnamed x18 -> x28, local copies, waits for them, and re-layouts: 2.48 us -> 11.1 us
    unnamed x5 -> x0, other arithmetic: 5.33 us -> none
    pallas_call x3, Pallas kernels: 24.4 us -> 27.7 us  [local_call(): pl.pallas_call(kernel, out_shape=[jax.ShapeDtypeStruct(shape, F32) for sh...]
    add x2 -> x0, other arithmetic: 1.52 us -> none  [pivots(): SCREENING + lax.dynamic_slice_in_dim(lam_x, start, count)[:, None]]
    ppermute x1 -> x0, starting transfers between devices: 1.29 us -> none  [local(): lax.ppermute(potential[0], 'tm', [(t, t - 1) for t in range(1, n)])]
    mul x1 -> x0, other arithmetic: 1.28 us -> none  [time_factors(): inverse(j0) * inverse(j0 + 1)]
  transfers between devices with their start and end apart: 1 -> 0, of which waited for: 0 -> 0; matrix products, arithmetic and copies ran while one was open for 8% -> 0% of each run, Pallas kernels for 0% -> 0%
where the time goes in v3:
time: 114 us
  Pallas kernels  102 us (89%)
  local copies, waits for them, and re-layouts  11.1 us (10%)
    pallas_call x2, Pallas kernels, solve(): pl.pallas_call(functools.partial(solve_kernel, n), out_shape=jax.ShapeDty...  74.5 us
    pallas_call x3, Pallas kernels, local_call(): pl.pallas_call(kernel, out_shape=[jax.ShapeDtypeStruct(shape, F32) for sh...  27.7 us
    unnamed x28, local copies, waits for them, and re-layouts  11.1 us

profile of v3, /device:TPU:0, one launch (start us, length us, event | category | flops | bytes accessed | tf_op | source)
XLA Modules:
  0.0 114.0 jit_solution(7950926953181853245)
XLA Ops:
  0.6 0.1 add_convert_fusion.flag
  0.7 1.2 %copy-done = bf16[2,512,512]{2,1,0:T(8,128)(2,1)S(1)} copy-done((bf16[2,512,512]{2,1,0:T(8,128)(2,1)S(1)}, bf16[2,512,512]{2,1,0:T(8,128)(2,1)}, u32[]{:S(2)}) %copy-start) | copy-done | bytes 1048600
  1.9 1.2 %copy-done.2 = bf16[2,512,512]{2,1,0:T(8,128)(2,1)S(1)} copy-done((bf16[2,512,512]{2,1,0:T(8,128)(2,1)S(1)}, bf16[2,512,512]{2,1,0:T(8,128)(2,1)}, u32[]{:S(2)}) %copy-start.2) | copy-done | bytes 1048600
  3.2 1.2 %copy-done.4 = f32[1,512,512]{2,1,0:T(8,128)S(1)} copy-done((f32[1,512,512]{2,1,0:T(8,128)S(1)}, f32[1,512,512]{2,1,0:T(8,128)}, u32[]{:S(2)}) %copy-start.4) | copy-done | bytes 1048600
  4.4 1.2 %copy-done.6 = f32[512,512]{1,0:T(8,128)S(1)} copy-done((f32[512,512]{1,0:T(8,128)S(1)}, f32[512,512]{1,0:T(8,128)}, u32[]{:S(2)}) %copy-start.6) | copy-done | bytes 1048600
  5.6 1.2 %copy-done.8 = f32[512,512]{1,0:T(8,128)S(1)} copy-done((f32[512,512]{1,0:T(8,128)S(1)}, f32[512,512]{1,0:T(8,128)}, u32[]{:S(2)}) %copy-start.8) | copy-done | bytes 1048600
  6.8 1.2 %copy-done.10 = f32[1,512,512]{2,1,0:T(8,128)S(1)} copy-done((f32[1,512,512]{2,1,0:T(8,128)S(1)}, f32[1,512,512]{2,1,0:T(8,128)}, u32[]{:S(2)}) %copy-start.10) | copy-done | bytes 1048600
  8.1 1.2 %copy-done.11 = f32[1,512,512]{2,1,0:T(8,128)S(1)} copy-done((f32[1,512,512]{2,1,0:T(8,128)S(1)}, f32[1,512,512]{2,1,0:T(8,128)}, u32[]{:S(2)}) %copy-start.11) | copy-done | bytes 1048600
  9.3 1.2 %copy-done.12 = f32[1,512,512]{2,1,0:T(8,128)S(1)} copy-done((f32[1,512,512]{2,1,0:T(8,128)S(1)}, f32[1,512,512]{2,1,0:T(8,128)}, u32[]{:S(2)}) %copy-start.12) | copy-done | bytes 1048600
  10.5 1.2 %copy-done.13 = f32[512,512]{1,0:T(8,128)S(1)} copy-done((f32[512,512]{1,0:T(8,128)S(1)}, f32[512,512]{1,0:T(8,128)}, u32[]{:S(2)}) %copy-start.13) | copy-done | bytes 1048600
  11.7 12.1 %shard_map.138 = (f32[512,512]{1,0:T(8,128)S(1)}, f32[512,512]{1,0:T(8,128)S(1)}, f32[512,512]{1,0:T(8,128)S(1)}, f32[2,512,512]{2,1,0:T(8,128)S(1)}, f32[512,51...) custom-call(f32[512,512]{1,0:T(8,128)S(1)} %bitcast.12, f32[512,512]{1,0:T(8,128)S(1)} %bitcast.13, ...), custom_call_target="tpu_custom_call" | custom-call | tf_op jit(solution)/shard_map/pallas_call | solution.py:483
  23.9 0.0 copy-start.1
  23.9 0.0 copy-start.3
  23.9 0.0 copy-start.5
  23.9 0.0 copy-start.7
  23.9 0.0 copy-start.9
  24.0 41.1 %shard_map.139.modes = f32[2,512,512]{2,1,0:T(8,128)S(1)} custom-call(f32[2,512,512]{2,1,0:T(8,128)S(1)} %get-tuple-element.16.wd, f32[6,256,512]{2,1,0:T(8,128)S(1)} %get-tuple-element.17.coef, f32[2,128,512]{2,1,0:T(8,128)S(1)} %get-tuple-element.18.other), custom_call_target="tpu_custom_call" | custom-call | tf_op jit(solution)/shard_map/pallas_call | solution.py:499
  65.1 0.0 copy-done.1
  65.1 0.0 copy-done.3
  65.1 0.0 copy-done.5
  65.1 0.0 copy-done.7
  65.1 12.6 %shard_map.140 = (f32[512,512]{1,0:T(8,128)}, f32[512,512]{1,0:T(8,128)}, f32[512,512]{1,0:T(8,128)}, f32[512,512]{1,0:T(8,128)S(1)}, f32[2,512,512]{2,1,0:T(8,128)S(1)}) custom-call(s32[2]{0:T(128)S(1)} %add_convert_fusion.flag, f32[2,512,512]{2,1,0:T(8,128)S(1)} %shard_map.139.modes, f32[512,512]{1,0:T(8,128)S(1)} %get-tuple-element.19.density, ...), custom_call_target="tpu_custom_call" | custom-call | tf_op jit(solution)/shard_map/pallas_call | solution.py:483
  77.7 33.4 %shard_map.141.modes = f32[2,512,512]{2,1,0:T(8,128)S(1)} custom-call(f32[2,512,512]{2,1,0:T(8,128)S(1)} %get-tuple-element.26.wd, f32[6,256,512]{2,1,0:T(8,128)S(1)} %get-tuple-element.17.coef, f32[2,128,512]{2,1,0:T(8,128)S(1)} %get-tuple-element.18.other), custom_call_target="tpu_custom_call" | custom-call | tf_op jit(solution)/shard_map/pallas_call | solution.py:499
  111.1 2.9 %shard_map.142 = f32[512,512]{1,0:T(8,128)} custom-call(f32[2,512,512]{2,1,0:T(8,128)S(1)} %shard_map.141.modes, f32[512,512]{1,0:T(8,128)S(1)} %get-tuple-element.27.pot, bf16[2,512,512]{2,1,0:T(8,128)(2,1)S(1)} %copy-done.1, bf16[2,512,512]{2,1,0:T(8,128)(2,1)S(1)} %copy-done.3), custom_call_target="tpu_custom_call" | custom-call | tf_op jit(solution)/shard_map/pallas_call | solution.py:483
  (10 shorter events, 0.0 us)
Async XLA Ops:
  0.7 1.2 %copy-start = (bf16[2,512,512]{2,1,0:T(8,128)(2,1)S(1)}, bf16[2,512,512]{2,1,0:T(8,128)(2,1)}, u32[]{:S(2)}) copy-start(bf16[2,512,512]{2,1,0:T(8,128)(2,1)} %constant.16.clone.tyt.txt) | copy-start | bytes 3145732
  1.9 1.2 %copy-start.2 = (bf16[2,512,512]{2,1,0:T(8,128)(2,1)S(1)}, bf16[2,512,512]{2,1,0:T(8,128)(2,1)}, u32[]{:S(2)}) copy-start(bf16[2,512,512]{2,1,0:T(8,128)(2,1)} %constant.15.clone.tx.ty) | copy-start | bytes 3145732
  3.2 1.2 %copy-start.4 = (f32[1,512,512]{2,1,0:T(8,128)S(1)}, f32[1,512,512]{2,1,0:T(8,128)}, u32[]{:S(2)}) copy-start(f32[1,512,512]{2,1,0:T(8,128)} %param.14) | copy-start | bytes 3145732
  4.4 1.2 %copy-start.6 = (f32[512,512]{1,0:T(8,128)S(1)}, f32[512,512]{1,0:T(8,128)}, u32[]{:S(2)}) copy-start(f32[512,512]{1,0:T(8,128)} %cost.3) | copy-start | bytes 3145732
  5.6 1.2 %copy-start.8 = (f32[512,512]{1,0:T(8,128)S(1)}, f32[512,512]{1,0:T(8,128)}, u32[]{:S(2)}) copy-start(f32[512,512]{1,0:T(8,128)} %init.3) | copy-start | bytes 3145732
  6.8 1.2 %copy-start.10 = (f32[1,512,512]{2,1,0:T(8,128)S(1)}, f32[1,512,512]{2,1,0:T(8,128)}, u32[]{:S(2)}) copy-start(f32[1,512,512]{2,1,0:T(8,128)} %param.11) | copy-start | bytes 3145732
  8.1 1.2 %copy-start.11 = (f32[1,512,512]{2,1,0:T(8,128)S(1)}, f32[1,512,512]{2,1,0:T(8,128)}, u32[]{:S(2)}) copy-start(f32[1,512,512]{2,1,0:T(8,128)} %param.12) | copy-start | bytes 3145732
  9.3 1.2 %copy-start.12 = (f32[1,512,512]{2,1,0:T(8,128)S(1)}, f32[1,512,512]{2,1,0:T(8,128)}, u32[]{:S(2)}) copy-start(f32[1,512,512]{2,1,0:T(8,128)} %param.13) | copy-start | bytes 3145732
  10.5 1.2 %copy-start.13 = (f32[512,512]{1,0:T(8,128)S(1)}, f32[512,512]{1,0:T(8,128)}, u32[]{:S(2)}) copy-start(f32[512,512]{1,0:T(8,128)} %constant.14.clone.mu) | copy-start | bytes 3145732
  23.9 41.2 %copy-start.1 = (bf16[2,512,512]{2,1,0:T(8,128)(2,1)S(1)}, bf16[2,512,512]{2,1,0:T(8,128)(2,1)}, u32[]{:S(2)}) copy-start(bf16[2,512,512]{2,1,0:T(8,128)(2,1)} %constant.16.clone.tyt.txt) | copy-start | bytes 3145732
  23.9 41.2 %copy-start.3 = (bf16[2,512,512]{2,1,0:T(8,128)(2,1)S(1)}, bf16[2,512,512]{2,1,0:T(8,128)(2,1)}, u32[]{:S(2)}) copy-start(bf16[2,512,512]{2,1,0:T(8,128)(2,1)} %constant.15.clone.tx.ty) | copy-start | bytes 3145732
  23.9 41.2 %copy-start.5 = (f32[1,512,512]{2,1,0:T(8,128)S(1)}, f32[1,512,512]{2,1,0:T(8,128)}, u32[]{:S(2)}) copy-start(f32[1,512,512]{2,1,0:T(8,128)} %param.14) | copy-start | bytes 3145732
  23.9 41.2 %copy-start.7 = (f32[512,512]{1,0:T(8,128)S(1)}, f32[512,512]{1,0:T(8,128)}, u32[]{:S(2)}) copy-start(f32[512,512]{1,0:T(8,128)} %cost.3) | copy-start | bytes 3145732
  23.9 41.2 %copy-start.9 = (f32[512,512]{1,0:T(8,128)S(1)}, f32[512,512]{1,0:T(8,128)}, u32[]{:S(2)}) copy-start(f32[512,512]{1,0:T(8,128)} %init.3) | copy-start | bytes 3145732

commit v4 on v3

--- a/solution.py
+++ b/solution.py
@@ -185,10 +185,15 @@
     lax.fori_loop(0, quarter // TILE, rest, 0)
 
 
-def first_kernel(
-    n, density, flux_x, flux_y, pot, cost, init, tx, tyt, mu,
-    o_d, o_x, o_y, hat, following, coef, other, work, mid, send, recv,
-):
+def first_kernel(n, *refs):
+    sources, (o_d, o_x, o_y, hat, following, coef, other) = refs[:9], refs[9:16]
+    work, mid, send, recv, load = refs[16:21]
+    held = refs[21:]
+    loads = [pltpu.make_async_copy(sources[j], held[j], load.at[j]) for j in range(9)]
+    for j in (8, 3, 0, 1, 2, 4, 5, 6, 7):
+        loads[j].start()
+    density, flux_x, flux_y, _, cost, init, tx, tyt, mu = held
+    pot = sources[3]
     me = lax.axis_index("tm")
     chunks = pot.shape[0] // TILE
     barrier = pltpu.get_barrier_semaphore()
@@ -218,7 +223,10 @@
     def _():
         lax.fori_loop(0, chunks, lambda k, c: (copy(k).start(), c)[1], 0)
 
+    loads[8].wait()
     factors(n, me, mu, coef, other)
+    for j in range(8):
+        loads[j].wait()
 
     def ready(k):
         @pl.when(me < n - 1)
@@ -226,7 +234,7 @@
             copy(k).wait_recv()
 
     forward_half(
-        me == 0, me == n - 1, (density, flux_x, flux_y), pot, following, cost, init, tx, tyt,
+        me == 0, me == n - 1, (density, flux_x, flux_y), held[3], following, cost, init, tx, tyt,
         (o_d, o_x, o_y), hat, work, mid, ready,
     )
 
@@ -474,6 +482,8 @@
 
 def local_call(kernel, inputs, outs, scratch, flag=None, collective=None):
     specs = vmem(len(inputs))
+    if collective is not None:
+        specs = [pl.BlockSpec(memory_space=pltpu.HBM)] * len(inputs)
     if flag is not None:
         specs = [pl.BlockSpec(memory_space=pltpu.SMEM)] + specs
         inputs = [flag] + inputs
@@ -534,7 +544,9 @@
         functools.partial(first_kernel, n),
         [density[0], flux_x[0], flux_y[0], potential[0], running_cost, initial_density, table_x, table_yt, mu],
         three + [hat_shape, shape, (6, rows // 2, cols), (2, rows // 4, cols)],
-        [work, mid, dma, dma], collective=1,
+        [work, mid, dma, dma, pltpu.SemaphoreType.DMA((9,))]
+        + [pltpu.VMEM(shape, F32)] * 6 + [mid, mid, pltpu.VMEM(shape, F32)],
+        collective=1,
     )
     modes = solve(n, hat, coef, other)
     d, fx, fy, pot, hat = local_call(

time: 114 us -> 115 us (level)
  no operation moved by 1% of the time
where the time goes in v4:
time: 115 us
  Pallas kernels  103 us (90%)
  local copies, waits for them, and re-layouts  11.1 us (10%)
    pallas_call x2, Pallas kernels, solve(): pl.pallas_call(functools.partial(solve_kernel, n), out_shape=jax.ShapeDty...  74.4 us
    pallas_call x3, Pallas kernels, local_call(): pl.pallas_call(kernel, out_shape=[jax.ShapeDtypeStruct(shape, F32) for sh...  28.4 us
    unnamed x28, local copies, waits for them, and re-layouts  11.1 us

profile of v4, /device:TPU:0, one launch (start us, length us, event | category | flops | bytes accessed | tf_op | source)
XLA Modules:
  0.0 114.7 jit_solution(9558617349762172147)
XLA Ops:
  0.6 0.1 add_convert_fusion.flag
  0.7 1.2 %copy-done = bf16[2,512,512]{2,1,0:T(8,128)(2,1)S(1)} copy-done((bf16[2,512,512]{2,1,0:T(8,128)(2,1)S(1)}, bf16[2,512,512]{2,1,0:T(8,128)(2,1)}, u32[]{:S(2)}) %copy-start) | copy-done | bytes 1048600
  1.9 1.2 %copy-done.2 = bf16[2,512,512]{2,1,0:T(8,128)(2,1)S(1)} copy-done((bf16[2,512,512]{2,1,0:T(8,128)(2,1)S(1)}, bf16[2,512,512]{2,1,0:T(8,128)(2,1)}, u32[]{:S(2)}) %copy-start.2) | copy-done | bytes 1048600
  3.2 1.2 %copy-done.4 = f32[1,512,512]{2,1,0:T(8,128)S(1)} copy-done((f32[1,512,512]{2,1,0:T(8,128)S(1)}, f32[1,512,512]{2,1,0:T(8,128)}, u32[]{:S(2)}) %copy-start.4) | copy-done | bytes 1048600
  4.4 1.2 %copy-done.6 = f32[512,512]{1,0:T(8,128)S(1)} copy-done((f32[512,512]{1,0:T(8,128)S(1)}, f32[512,512]{1,0:T(8,128)}, u32[]{:S(2)}) %copy-start.6) | copy-done | bytes 1048600
  5.6 1.2 %copy-done.8 = f32[512,512]{1,0:T(8,128)S(1)} copy-done((f32[512,512]{1,0:T(8,128)S(1)}, f32[512,512]{1,0:T(8,128)}, u32[]{:S(2)}) %copy-start.8) | copy-done | bytes 1048600
  6.8 1.2 %copy-done.10 = f32[1,512,512]{2,1,0:T(8,128)S(1)} copy-done((f32[1,512,512]{2,1,0:T(8,128)S(1)}, f32[1,512,512]{2,1,0:T(8,128)}, u32[]{:S(2)}) %copy-start.10) | copy-done | bytes 1048600
  8.1 1.2 %copy-done.11 = f32[1,512,512]{2,1,0:T(8,128)S(1)} copy-done((f32[1,512,512]{2,1,0:T(8,128)S(1)}, f32[1,512,512]{2,1,0:T(8,128)}, u32[]{:S(2)}) %copy-start.11) | copy-done | bytes 1048600
  9.3 1.2 %copy-done.12 = f32[1,512,512]{2,1,0:T(8,128)S(1)} copy-done((f32[1,512,512]{2,1,0:T(8,128)S(1)}, f32[1,512,512]{2,1,0:T(8,128)}, u32[]{:S(2)}) %copy-start.12) | copy-done | bytes 1048600
  10.5 1.2 %copy-done.13 = f32[512,512]{1,0:T(8,128)S(1)} copy-done((f32[512,512]{1,0:T(8,128)S(1)}, f32[512,512]{1,0:T(8,128)}, u32[]{:S(2)}) %copy-start.13) | copy-done | bytes 1048600
  11.7 12.9 %shard_map.138 = (f32[512,512]{1,0:T(8,128)S(1)}, f32[512,512]{1,0:T(8,128)S(1)}, f32[512,512]{1,0:T(8,128)S(1)}, f32[2,512,512]{2,1,0:T(8,128)S(1)}, f32[512,51...) custom-call(f32[512,512]{1,0:T(8,128)S(1)} %bitcast.12, f32[512,512]{1,0:T(8,128)S(1)} %bitcast.13, ...), custom_call_target="tpu_custom_call" | custom-call | tf_op jit(solution)/shard_map/pallas_call | solution.py:493
  24.6 0.0 copy-start.1
  24.6 0.0 copy-start.3
  24.6 0.0 copy-start.5
  24.7 0.0 copy-start.7
  24.7 0.0 copy-start.9
  24.7 41.1 %shard_map.139.modes = f32[2,512,512]{2,1,0:T(8,128)S(1)} custom-call(f32[2,512,512]{2,1,0:T(8,128)S(1)} %get-tuple-element.16.wd, f32[6,256,512]{2,1,0:T(8,128)S(1)} %get-tuple-element.17.coef, f32[2,128,512]{2,1,0:T(8,128)S(1)} %get-tuple-element.18.other), custom_call_target="tpu_custom_call" | custom-call | tf_op jit(solution)/shard_map/pallas_call | solution.py:509
  65.8 0.0 copy-done.1
  65.8 0.0 copy-done.3
  65.8 0.0 copy-done.5
  65.8 0.0 copy-done.7
  65.9 12.6 %shard_map.140 = (f32[512,512]{1,0:T(8,128)}, f32[512,512]{1,0:T(8,128)}, f32[512,512]{1,0:T(8,128)}, f32[512,512]{1,0:T(8,128)S(1)}, f32[2,512,512]{2,1,0:T(8,128)S(1)}) custom-call(s32[2]{0:T(128)S(1)} %add_convert_fusion.flag, f32[2,512,512]{2,1,0:T(8,128)S(1)} %shard_map.139.modes, f32[512,512]{1,0:T(8,128)S(1)} %get-tuple-element.19.density, ...), custom_call_target="tpu_custom_call" | custom-call | tf_op jit(solution)/shard_map/pallas_call | solution.py:493
  78.5 33.3 %shard_map.141.modes = f32[2,512,512]{2,1,0:T(8,128)S(1)} custom-call(f32[2,512,512]{2,1,0:T(8,128)S(1)} %get-tuple-element.26.wd, f32[6,256,512]{2,1,0:T(8,128)S(1)} %get-tuple-element.17.coef, f32[2,128,512]{2,1,0:T(8,128)S(1)} %get-tuple-element.18.other), custom_call_target="tpu_custom_call" | custom-call | tf_op jit(solution)/shard_map/pallas_call | solution.py:509
  111.8 2.9 %shard_map.142 = f32[512,512]{1,0:T(8,128)} custom-call(f32[2,512,512]{2,1,0:T(8,128)S(1)} %shard_map.141.modes, f32[512,512]{1,0:T(8,128)S(1)} %get-tuple-element.27.pot, bf16[2,512,512]{2,1,0:T(8,128)(2,1)S(1)} %copy-done.1, bf16[2,512,512]{2,1,0:T(8,128)(2,1)S(1)} %copy-done.3), custom_call_target="tpu_custom_call" | custom-call | tf_op jit(solution)/shard_map/pallas_call | solution.py:493
  (10 shorter events, 0.0 us)
Async XLA Ops:
  0.7 1.2 %copy-start = (bf16[2,512,512]{2,1,0:T(8,128)(2,1)S(1)}, bf16[2,512,512]{2,1,0:T(8,128)(2,1)}, u32[]{:S(2)}) copy-start(bf16[2,512,512]{2,1,0:T(8,128)(2,1)} %constant.16.clone.refs_7_.txt.tyt) | copy-start | bytes 3145732
  1.9 1.2 %copy-start.2 = (bf16[2,512,512]{2,1,0:T(8,128)(2,1)S(1)}, bf16[2,512,512]{2,1,0:T(8,128)(2,1)}, u32[]{:S(2)}) copy-start(bf16[2,512,512]{2,1,0:T(8,128)(2,1)} %constant.15.clone.refs_6_.tx.ty) | copy-start | bytes 3145732
  3.2 1.2 %copy-start.4 = (f32[1,512,512]{2,1,0:T(8,128)S(1)}, f32[1,512,512]{2,1,0:T(8,128)}, u32[]{:S(2)}) copy-start(f32[1,512,512]{2,1,0:T(8,128)} %param.14) | copy-start | bytes 3145732
  4.4 1.2 %copy-start.6 = (f32[512,512]{1,0:T(8,128)S(1)}, f32[512,512]{1,0:T(8,128)}, u32[]{:S(2)}) copy-start(f32[512,512]{1,0:T(8,128)} %cost.1) | copy-start | bytes 3145732
  5.6 1.2 %copy-start.8 = (f32[512,512]{1,0:T(8,128)S(1)}, f32[512,512]{1,0:T(8,128)}, u32[]{:S(2)}) copy-start(f32[512,512]{1,0:T(8,128)} %init.1) | copy-start | bytes 3145732
  6.8 1.2 %copy-start.10 = (f32[1,512,512]{2,1,0:T(8,128)S(1)}, f32[1,512,512]{2,1,0:T(8,128)}, u32[]{:S(2)}) copy-start(f32[1,512,512]{2,1,0:T(8,128)} %param.11) | copy-start | bytes 3145732
  8.1 1.2 %copy-start.11 = (f32[1,512,512]{2,1,0:T(8,128)S(1)}, f32[1,512,512]{2,1,0:T(8,128)}, u32[]{:S(2)}) copy-start(f32[1,512,512]{2,1,0:T(8,128)} %param.12) | copy-start | bytes 3145732
  9.3 1.2 %copy-start.12 = (f32[1,512,512]{2,1,0:T(8,128)S(1)}, f32[1,512,512]{2,1,0:T(8,128)}, u32[]{:S(2)}) copy-start(f32[1,512,512]{2,1,0:T(8,128)} %param.13) | copy-start | bytes 3145732
  10.5 1.2 %copy-start.13 = (f32[512,512]{1,0:T(8,128)S(1)}, f32[512,512]{1,0:T(8,128)}, u32[]{:S(2)}) copy-start(f32[512,512]{1,0:T(8,128)} %constant.14.clone.refs_8_) | copy-start | bytes 3145732
  24.6 41.2 %copy-start.1 = (bf16[2,512,512]{2,1,0:T(8,128)(2,1)S(1)}, bf16[2,512,512]{2,1,0:T(8,128)(2,1)}, u32[]{:S(2)}) copy-start(bf16[2,512,512]{2,1,0:T(8,128)(2,1)} %constant.16.clone.refs_7_.txt.tyt) | copy-start | bytes 3145732
  24.6 41.2 %copy-start.3 = (bf16[2,512,512]{2,1,0:T(8,128)(2,1)S(1)}, bf16[2,512,512]{2,1,0:T(8,128)(2,1)}, u32[]{:S(2)}) copy-start(bf16[2,512,512]{2,1,0:T(8,128)(2,1)} %constant.15.clone.refs_6_.tx.ty) | copy-start | bytes 3145732
  24.6 41.2 %copy-start.5 = (f32[1,512,512]{2,1,0:T(8,128)S(1)}, f32[1,512,512]{2,1,0:T(8,128)}, u32[]{:S(2)}) copy-start(f32[1,512,512]{2,1,0:T(8,128)} %param.14) | copy-start | bytes 3145732
  24.7 41.2 %copy-start.7 = (f32[512,512]{1,0:T(8,128)S(1)}, f32[512,512]{1,0:T(8,128)}, u32[]{:S(2)}) copy-start(f32[512,512]{1,0:T(8,128)} %cost.1) | copy-start | bytes 3145732
  24.7 41.2 %copy-start.9 = (f32[512,512]{1,0:T(8,128)S(1)}, f32[512,512]{1,0:T(8,128)}, u32[]{:S(2)}) copy-start(f32[512,512]{1,0:T(8,128)} %init.1) | copy-start | bytes 3145732
